TPU v7x, 256 devices: a whole 4x4x8 slice. The times are simulated.
256 devices in a mesh: dp: 16 (over z_lo, x), mp: 16 (over z_hi, y, core).
Axes of the slice: x: 4, y: 4, z: 8 (z_hi: 2, z_lo: 4; z = z_hi * 4 + z_lo), core: 2. Of those that a mesh axis runs over, the one named last changes fastest.
Arguments:
- field: bfloat16 [16, 32, 128, 64, 128], P('dp', None, 'mp'), may hold values from -6 to 6
- cotangent: bfloat16 [16, 32, 128, 64, 128], P('dp', None, 'mp'), may hold values from -6 to 6
- spectral_weight: float32 [32, 32, 32, 32, 32], P('mp', 'dp'), may hold values from -6 to 6
- first_moment: float32 [32, 32, 32, 32, 32], P('mp', 'dp'), may hold values from -4.2 to 4.2
- second_moment: float32 [32, 32, 32, 32, 32], P('mp', 'dp'), may hold values from 4 to 64
- local_weight: bfloat16 [32, 32], replicated, may hold values from -1 to 1
Outputs:
- new_weight: float32 [32, 32, 32, 32, 32], P('mp', 'dp')
- new_first: float32 [32, 32, 32, 32, 32], P('mp', 'dp')
- new_second: float32 [32, 32, 32, 32, 32], P('mp', 'dp')
All inputs are finite; a program needn't handle non-finite values.
Results may differ from a plain program's by a relative error of at most 0.02.
Values may be sent and summed in bfloat16 or wider, within the bound.
No kernel may reach another device: no remote copies, remote signals or barrier semaphores. Data moves between devices by JAX's collectives and lax.ppermute only.
A program may use at most 192 MiB of HBM per device.

v0:
```python
import jax
import jax.numpy as jnp
from jax import lax
from jax.sharding import PartitionSpec as P

beta_one = 0.9
beta_two = 0.999
learn_rate = 0.001
decay_rate = 0.1
adam_eps = 1e-08
adam_step = 1000.0


def table(length, modes):
    grid = jnp.arange(length, dtype=jnp.float32)[:, None]
    index = jnp.arange(2 * modes, dtype=jnp.float32)[None, :]
    freq = jnp.where(index < modes, index, index - modes + 1.0)
    phase = 2.0 * jnp.pi * freq * grid / length
    values = jnp.where(index < modes, jnp.cos(phase), jnp.sin(phase)) * jnp.sqrt(2.0 / length)
    return values.astype(jnp.bfloat16)


def project_onto_modes(block, cosine_sine_x_table, cosine_sine_y_table, cosine_sine_z_table):
    first = jnp.einsum(
        "sczxy,yb->sczxb", block, cosine_sine_y_table, preferred_element_type=jnp.float32
    ).astype(jnp.bfloat16)
    second = jnp.einsum(
        "sczxb,xa->sczab", first, cosine_sine_x_table, preferred_element_type=jnp.float32
    ).astype(jnp.bfloat16)
    moved = lax.all_to_all(second, "mp", split_axis=3, concat_axis=2, tiled=True)
    return jnp.einsum(
        "sczab,zk->scabk", moved, cosine_sine_z_table, preferred_element_type=jnp.float32
    ).astype(jnp.bfloat16)


def from_modes(coeffs, cosine_sine_x_table, cosine_sine_y_table, cosine_sine_z_table):
    depth = jnp.einsum(
        "scabk,zk->sczab", coeffs, cosine_sine_z_table, preferred_element_type=jnp.float32
    ).astype(jnp.bfloat16)
    moved = lax.all_to_all(depth, "mp", split_axis=2, concat_axis=3, tiled=True)
    second = jnp.einsum(
        "sczab,xa->sczxb", moved, cosine_sine_x_table, preferred_element_type=jnp.float32
    ).astype(jnp.bfloat16)
    return jnp.einsum(
        "sczxb,yb->sczxy", second, cosine_sine_y_table, preferred_element_type=jnp.float32
    )


def body(field, cotangent, spectral_weight, first_moment, second_moment, local_weight):
    depth_total = field.shape[2] * lax.axis_size("mp")
    modes_half = spectral_weight.shape[2] // 2
    cosine_sine_x_table = table(field.shape[3], modes_half)
    cosine_sine_y_table = table(field.shape[4], modes_half)
    cosine_sine_z_table = table(depth_total, modes_half)
    lowest_mode_weight = spectral_weight.astype(jnp.bfloat16)
    input_spectrum = project_onto_modes(
        field, cosine_sine_x_table, cosine_sine_y_table, cosine_sine_z_table
    )
    output_spectrum = jnp.einsum(
        "wrydf,ydfrn->wnydf",
        input_spectrum,
        lax.all_gather(lowest_mode_weight, "dp", axis=1, tiled=True),
        preferred_element_type=jnp.float32,
    ).astype(jnp.bfloat16)
    spectral = from_modes(
        output_spectrum, cosine_sine_x_table, cosine_sine_y_table, cosine_sine_z_table
    )
    local = jnp.einsum("sczxy,co->sozxy", field, local_weight, preferred_element_type=jnp.float32)
    pre = spectral + local
    unused, pull = jax.vjp(jax.nn.gelu, pre)
    grad_pre = pull(cotangent.astype(jnp.float32))[0].astype(jnp.bfloat16)
    gradient_spectrum = project_onto_modes(
        grad_pre, cosine_sine_x_table, cosine_sine_y_table, cosine_sine_z_table
    )
    summed = lax.psum_scatter(
        jnp.einsum(
            "nvtxy,netxy->xtyve",
            input_spectrum,
            gradient_spectrum,
            preferred_element_type=jnp.float32,
        ).astype(jnp.bfloat16),
        "dp",
        scatter_dimension=0,
        tiled=True,
    ).astype(jnp.float32)
    weight_gradient = jnp.transpose(summed, (1, 0, 2, 3, 4))
    new_first = beta_one * first_moment + (1.0 - beta_one) * weight_gradient
    new_second = beta_two * second_moment + (1.0 - beta_two) * weight_gradient * weight_gradient
    first_hat = new_first / (1.0 - beta_one**adam_step)
    second_hat = new_second / (1.0 - beta_two**adam_step)
    new_weight = spectral_weight - learn_rate * (
        first_hat / (jnp.sqrt(second_hat) + adam_eps) + decay_rate * spectral_weight
    )
    return (new_weight, new_first, new_second)


def solution(mesh):
    in_specs = (
        P("dp", None, "mp", None, None),
        P("dp", None, "mp", None, None),
        P("mp", "dp", None, None, None),
        P("mp", "dp", None, None, None),
        P("mp", "dp", None, None, None),
        P(),
    )
    out_specs = (
        P("mp", "dp", None, None, None),
        P("mp", "dp", None, None, None),
        P("mp", "dp", None, None, None),
    )
    return jax.shard_map(body, mesh=mesh, in_specs=in_specs, out_specs=out_specs, check_vma=False)
```

profile of v0, /device:TPU:1, one launch (start us, length us, event | category | flops | bytes accessed | tf_op | source)
XLA Modules:
  0.0 729.4 jit_solution(2868507002727601442)
XLA Ops:
  7.2 0.0 copy-start
  7.2 0.0 all-gather.2.cloned.1.call-start
  7.2 2.8 convert_element_type.107
  10.0 0.0 all-gather.2.cloned.1.call-update
  10.1 10.8 %convert_bitcast_fusion.1 = bf16[1,32,8,32,32]{4,3,2,1,0:T(8,128)(2,1)} fusion(f32[32]{0:T(128)S(1)} %fusion.101, pred[32]{0:T(512)(128)(4,1)S(1)} %iota_compare_fusion, bf16[1,32,8,64,128]{4,3,2,1,0:T(8,128)(2,1)} %param.6), kind=kOutput, calls=%fused_computation.44 | convolution fusion | flops 168589312 | bytes 4718752 | tf_op jit(solution)/shard_map/sczxb,xa->sczab/dot_general | solution.py:27
  20.8 2.4 copy.93
  23.2 2.0 reshape.106
  25.2 32.4 %all_to_all.45 = bf16[16,2,8192]{2,1,0:T(2,128)(2,1)S(1)} all-to-all(bf16[16,2,8192]{2,1,0:T(2,128)(2,1)S(1)} %reshape.106), channel_id=1, replica_groups=mesh['dp'=16,'mp'=16] {'mp'}, dimensions={0} | all-to-all | bytes 1048576 | tf_op jit(solution)/shard_map/all_to_all | solution.py:30
  57.6 1.0 reshape.107
  58.7 1.7 convert_bitcast_fusion.2
  60.4 1.7 copy.58
  62.1 145.4 %all-gather.2.cloned.1.call-done = bf16[2,32,32,32,32]{4,3,2,1,0:T(8,128)(2,1)} async-done(((bf16[2,2,32,32,32]{4,3,2,1,0:T(8,128)(2,1)}), bf16[2,32,32,32,32]{4,3,2,1,0:T(8,128)(2,1)}) %all-gather.2.cloned.1.call-update) | async-done | bytes 4194320 | tf_op jit(solution)/shard_map/all_gather | solution.py:62
  207.5 12.8 %multiply_reduce_fusion = bf16[2,32,32,32]{3,2,1,0:T(8,128)(2,1)S(1)} fusion(bf16[2,32,32,32,32]{4,3,2,1,0:T(8,128)(2,1)} %all-gather.2.cloned.1.call-done, f32[2,32,32,32]{3,2,1,0:T(8,128)S(1)} %copy.58), kind=kLoop, calls=%fused_computation | loop fusion | flops 6225920 | bytes 4587520
  220.4 0.9 copy.52
  221.2 1.2 fusion.55
  222.4 4.6 copy.33
  227.0 2.7 reshape.108
  229.7 19.8 %all-to-all-start.1 = ((bf16[16,2,8192]{2,1,0:T(2,128)(2,1)}), bf16[16,2,8192]{2,1,0:T(2,128)(2,1)}, u32[]{:S(2)}, u32[]{:S(2)}) async-start(bf16[16,2,8192]{2,1,0:T(2,128)(2,1)} %reshape.108), calls=%async_computation.1 | async-start | bytes 1048576 | tf_op jit(solution)/shard_map/all_to_all | solution.py:40
  249.6 0.0 copy-done
  249.6 8.0 %fusion.13 = f32[32,8,64,128]{3,0,2,1:T(8,128)} fusion(bf16[32,8,64,128]{3,2,1,0:T(8,128)(2,1)} %bitcast.147, bf16[32,32]{1,0:T(8,128)(2,1)S(1)} %copy-done), kind=kOutput, calls=%fused_computation.20 | convolution fusion | flops 134217728 | bytes 12584960 | tf_op jit(solution)/shard_map/sczxy,co->sozxy/dot_general | solution.py:68
  257.6 5.6 all-to-all-done.1
  263.2 5.1 reshape.109
  268.3 2.4 copy.91
  270.7 0.4 copy.35
  271.1 1.0 fusion.29
  272.1 19.0 %fusion.11 = bf16[32,8,64,32]{2,3,1,0:T(8,128)(2,1)} fusion(bf16[1,32,8,64,128]{4,3,2,1,0:T(8,128)(2,1)} %param.7, f32[32,8,64,128]{3,0,2,1:T(8,128)} %fusion.13, bf16[64,32,8,32]{0,3,2,1:T(8,128)(2,1)S(1)} %fusion.29, f32[32]{0:T(128)S(1)} %fusion.101, pred[32]{0:T(512)(128)(4,1)S(1)} %iota_compare_fusion), kind=kOutput, calls=%fused_computation.18 | convolution fusion | flops 314613760 | bytes 14680224 | tf_op jit(solution)/shard_map/sczxy,yb->sczxb/dot_general | solution.py:24
  291.2 4.9 convert_bitcast_fusion
  296.0 0.8 copy.92
  296.9 2.7 reshape.110
  299.6 5.1 all-to-all-start.2
  304.7 0.0 all-reduce.3.cloned.1.call-start
  304.7 1.6 copy.32
  306.3 12.3 %all-to-all-done.2 = bf16[16,2,8192]{2,1,0:T(2,128)(2,1)} async-done(((bf16[16,2,8192]{2,1,0:T(2,128)(2,1)}), bf16[16,2,8192]{2,1,0:T(2,128)(2,1)}, u32[]{:S(2)}, u32[]{:S(2)}) %all-to-all-start.2) | async-done | bytes 524320 | tf_op jit(solution)/shard_map/all_to_all | solution.py:30
  318.6 3.3 reshape.111
  321.9 0.0 copy-start.3
  321.9 1.7 fusion.52
  323.6 1.7 copy.43
  325.3 0.0 copy-done.3
  325.3 11.1 %multiply_convert_fusion = bf16[32,2,32,32,32]{4,3,2,0,1:T(8,128)(2,1)} fusion(f32[32,2,32,32]{3,2,0,1:T(8,128)S(1)} %copy.43, f32[32,2,32,32]{3,2,0,1:T(8,128)S(1)} %copy-done.3), kind=kLoop, calls=%fused_computation.1 | loop fusion | flops 4194304 | bytes 4718592 | tf_op jit(solution)/shard_map/convert_element_type | solution.py:81
  336.4 0.0 copy-start.4
  336.4 0.0 copy-start.2
  336.4 0.0 all-reduce.3.cloned.1.call-update
  336.5 0.6 copy-done.4
  337.1 0.6 dynamic-slice
  338.3 377.3 %all-reduce.3.cloned.1.call-done = bf16[32,2,32,32,32]{4,3,2,0,1:T(8,128)(2,1)} async-done(((bf16[32,2,32,32,32]{4,3,2,0,1:T(8,128)(2,1)}), bf16[32,2,32,32,32]{4,3,2,0,1:T(8,128)(2,1)}) %all-reduce.3.cloned.1.call-update) | async-done | bytes 4194320
  715.7 0.0 copy-done.2
  715.7 0.0 copy-start.1
  715.7 6.4 multiply_subtract_fusion
  722.1 0.0 copy-done.1
  (2 shorter events, 0.0 us)
Async XLA Ops:
  7.2 242.4 %copy-start = (bf16[32,32]{1,0:T(8,128)(2,1)S(1)}, bf16[32,32]{1,0:T(8,128)(2,1)}, u32[]{:S(2)}) copy-start(bf16[32,32]{1,0:T(8,128)(2,1)} %param.11) | copy-start | bytes 6148
  7.2 200.3 %all-gather.2.cloned.1.call-start = ((), (), s32[]{:S(2)}) async-start(), calls=%async_computation.3 | async-start | bytes 17825792 | tf_op jit(solution)/shard_map/all_gather | solution.py:62
  229.7 33.5 %all-to-all-start.1 = ((bf16[16,2,8192]{2,1,0:T(2,128)(2,1)}), bf16[16,2,8192]{2,1,0:T(2,128)(2,1)}, u32[]{:S(2)}, u32[]{:S(2)}) async-start(bf16[16,2,8192]{2,1,0:T(2,128)(2,1)} %reshape.108), calls=%async_computation.1 | async-start | bytes 1048576 | tf_op jit(solution)/shard_map/all_to_all | solution.py:40
  299.6 19.0 %all-to-all-start.2 = ((bf16[16,2,8192]{2,1,0:T(2,128)(2,1)}), bf16[16,2,8192]{2,1,0:T(2,128)(2,1)}, u32[]{:S(2)}, u32[]{:S(2)}) async-start(bf16[16,2,8192]{2,1,0:T(2,128)(2,1)} %reshape.110), calls=%async_computation.2 | async-start | bytes 1048576 | tf_op jit(solution)/shard_map/all_to_all | solution.py:30
  304.7 411.0 %all-reduce.3.cloned.1.call-start = ((), (), s32[]{:S(2)}) async-start(), calls=%async_computation.4 | async-start | bytes 33554432
  321.9 3.5 copy-start.3
  336.4 0.7 copy-start.4
  336.4 379.2 %copy-start.2 = (f32[2,2,32,32,32]{4,3,2,1,0:T(8,128)S(1)}, f32[2,2,32,32,32]{4,3,2,1,0:T(8,128)}, u32[]{:S(2)}) copy-start(f32[2,2,32,32,32]{4,3,2,1,0:T(8,128)} %param.8) | copy-start | bytes 1572868
  715.7 6.4 copy-start.1
Sparse Core Ops, SparseCore 0:
  10.4 197.0 all-gather.1
  336.6 379.0 all-reduce.2
where the time goes:
time: 738 us; the launch traced here: 729 us
  waiting for transfers between devices  541 us (73%)
  matrix products  48.3 us (7%)
  local copies, waits for them, and re-layouts  34.6 us (5%)
  other arithmetic  33.1 us (4%)
  blocking collectives  32.4 us (4%)
  starting transfers between devices  25 us (3%)
  between operations  15.3 us (2%)
    unnamed x3, waiting for transfers between devices  377 us
    all_gather x1, waiting for transfers between devices, body(): lax.all_gather(lowest_mode_weight, 'dp', axis=1, tiled=True)  145 us
    all_to_all x1, blocking collectives, project_onto_modes(): lax.all_to_all(second, 'mp', split_axis=3, concat_axis=2, tiled=True)  32.4 us
    all_to_all x1, starting transfers between devices, from_modes(): moved = lax.all_to_all(depth, 'mp', split_axis=2, concat_axis=3, tiled=True)  19.8 us
    unnamed x18, local copies, waits for them, and re-layouts  19.8 us
    dot_general x1, matrix products, project_onto_modes(): jnp.einsum('sczxy,yb->sczxb', block, cosine_sine_y_table, preferred_eleme...  19 us
    dot_general x2, matrix products, project_onto_modes(): jnp.einsum('sczxb,xa->sczab', first, cosine_sine_x_table, preferred_eleme...  15.6 us
  transfers between devices with their start and end apart: 4, of which 4 were waited for; matrix products, arithmetic and copies ran while one was open for 4% of the time, Pallas kernels for 0%

commit v1 on v0

v1 whole, which is shorter than its diff:
```python
import jax
import jax.numpy as jnp
import ml_dtypes
import numpy as np
from jax import lax
from jax.experimental import pallas as pl
from jax.experimental.pallas import tpu as pltpu
from jax.sharding import PartitionSpec as P

beta_one = 0.9
beta_two = 0.999
learn_rate = 0.001
decay_rate = 0.1
adam_eps = 1e-08
adam_step = 1000.0

F32 = jnp.float32
BF16 = jnp.bfloat16
VMEM = 40 * 1024 * 1024


def table(length, modes=16):
    grid = np.arange(length, dtype=np.float32)[:, None]
    index = np.arange(2 * modes, dtype=np.float32)[None, :]
    freq = np.where(index < modes, index, index - np.float32(modes - 1)).astype(np.float32)
    phase = (np.float32(2.0 * np.pi) * freq * grid / np.float32(length)).astype(np.float32)
    values = np.where(index < modes, np.cos(phase), np.sin(phase)) * np.sqrt(np.float32(2.0 / length))
    return values.astype(np.float32).astype(ml_dtypes.bfloat16).astype(np.float32)


def constants():
    bx, by, bz = table(64), table(128), table(128)
    left_x = np.einsum("xa,cd->acdx", bx, np.eye(8, dtype=np.float32)).reshape(256, 512)
    by_rows = by.T.reshape(16, 2, 128).transpose(1, 0, 2).reshape(32, 128)
    by_blocks = np.kron(np.eye(4, dtype=np.float32), by_rows)
    left_z = np.einsum(
        "nqtk,bd->btkndq", bz.reshape(16, 4, 2, 32), np.eye(2, dtype=np.float32)
    ).reshape(128, 128)
    low = lambda v: jnp.asarray(np.ascontiguousarray(v).astype(ml_dtypes.bfloat16))
    return low(left_x), low(left_x.T), low(by_rows), low(by_blocks), low(left_z), low(left_z.T)


def dot(a, b):
    return lax.dot_general(a, b, (((1,), (0,)), ((), ())), preferred_element_type=F32)


def dot_nt(a, b):
    return lax.dot_general(a, b, (((1,), (1,)), ((), ())), preferred_element_type=F32)


def whole(shape):
    zeros = (0,) * len(shape)
    return pl.BlockSpec(shape, lambda i: zeros)


def call(kernel, grid, in_specs, out_specs, out_shape, scratch, flops, name):
    return pl.pallas_call(
        kernel,
        grid=(grid,),
        in_specs=in_specs,
        out_specs=out_specs,
        out_shape=out_shape,
        scratch_shapes=scratch,
        compiler_params=pltpu.CompilerParams(vmem_limit_bytes=VMEM),
        cost_estimate=pl.CostEstimate(flops=flops, bytes_accessed=8 << 20, transcendentals=0),
        name=name,
    )


def store_x_modes(first, group, product):
    split = product.reshape(16, 2, 8, 256)
    for z2 in range(2):
        first[:, z2, :, group] = split[:, :, :, z2 * 128 : (z2 + 1) * 128]


def y_modes_to_messages(first, by_rows, messages, zq):
    rows = first[...].reshape(2048, 128).astype(BF16)
    planar = dot_nt(by_rows, rows)
    for ap in range(16):
        for b2 in range(2):
            messages[pl.ds(ap * 8 + b2 * 4 + zq, 16, stride=128), :] = planar[
                b2 * 16 : (b2 + 1) * 16, ap * 128 : (ap + 1) * 128
            ]


def forward_kernel(field, left_x, by_rows, out, first, messages):
    zq = pl.program_id(0)
    for group in range(4):
        block = jnp.concatenate(
            [field[0, group * 8 : (group + 1) * 8, z2].reshape(512, 128) for z2 in range(2)], axis=1
        )
        store_x_modes(first, group, dot(left_x[...], block))
    y_modes_to_messages(first, by_rows[...], messages, zq)

    @pl.when(zq == 3)
    def _():
        out[...] = messages[...].astype(BF16)


def forward(field, left_x, by_rows):
    return call(
        forward_kernel,
        4,
        [
            pl.BlockSpec((1, 32, 2, 64, 128), lambda i: (0, 0, i, 0, 0)),
            whole((256, 512)),
            whole((32, 128)),
        ],
        whole((2048, 128)),
        jax.ShapeDtypeStruct((2048, 128), BF16),
        [pltpu.VMEM((16, 2, 2, 4, 8, 128), F32), pltpu.VMEM((2048, 128), F32)],
        1 << 31,
        "planes_to_modes",
    )(field, left_x, by_rows)


def local_kernel(field, left_c, out):
    for xg in range(4):
        cols = []
        for z2 in range(2):
            rows = field[0, :, z2, xg * 16 : (xg + 1) * 16, :].astype(F32)
            cols.append(rows.reshape(32, 2, 8, 128))
        halves = []
        for half in range(2):
            block = jnp.concatenate([c[:, half].reshape(256, 128) for c in cols], axis=1)
            halves.append(dot(left_c[...], block.astype(BF16)))
        for z2 in range(2):
            parts = [h[:, z2 * 128 : (z2 + 1) * 128].reshape(32, 1, 8, 128) for h in halves]
            both = jnp.concatenate(parts, axis=1).reshape(32, 16, 128)
            out[0, :, z2, xg * 16 : (xg + 1) * 16, :] = both.astype(BF16)


def local_mix(field, left_c):
    plane = pl.BlockSpec((1, 32, 2, 64, 128), lambda i: (0, 0, i, 0, 0))
    return call(
        local_kernel,
        4,
        [plane, whole((256, 256))],
        plane,
        jax.ShapeDtypeStruct(field.shape, BF16),
        [],
        1 << 31,
        "local_mix",
    )(field, left_c)


def spread_kernel(weight, out):
    row = lax.broadcasted_iota(jnp.int32, (32, 128), 0)
    lane = lax.broadcasted_iota(jnp.int32, (32, 128), 1)
    for b2 in range(2):
        for a2 in range(2):
            r = b2 * 2 + a2
            shift = jnp.where(lane == row + 32 * r, 1.0, 0.0).astype(BF16)
            rows = weight[a2, b2].reshape(256, 32).astype(BF16)
            out[:, r * 32 : (r + 1) * 32, :] = dot(rows, shift).astype(BF16).reshape(8, 32, 128)


def spread_weights(weight):
    return call(
        spread_kernel,
        4,
        [pl.BlockSpec((2, 2, 8, 32, 32), lambda i: (0, 0, i, 0, 0))],
        pl.BlockSpec((8, 128, 128), lambda i: (i, 0, 0)),
        jax.ShapeDtypeStruct((32, 128, 128), BF16),
        [],
        1 << 28,
        "spread_weights",
    )(weight)


def z_modes(received, left_z, spectrum):
    low_half = lax.broadcasted_iota(jnp.int32, (32, 128), 1) < 64
    for s in range(16):
        p = dot(left_z, received[s * 128 : (s + 1) * 128, :])
        stay = jnp.where(low_half, p[0:32], p[96:128])
        move = jnp.where(low_half, p[64:96], p[32:64])
        spectrum[pl.ds(s, 32, stride=16), :] = stay + pltpu.roll(move, 64, axis=1)


def mix_kernel(received, weights, left_z, right_z, out, kept, spectrum, mixed):
    z_modes(received, left_z[...], spectrum)
    kept[...] = spectrum[...].astype(BF16)
    for k in range(32):
        rows = slice(k * 16, (k + 1) * 16)
        mixed[rows, :] = dot(spectrum[rows, :].astype(BF16), weights[k])
    low_half = lax.broadcasted_iota(jnp.int32, (32, 128), 1) < 64
    for s in range(16):
        y = mixed[pl.ds(s, 32, stride=16), :]
        turned = pltpu.roll(y, 64, axis=1)
        stack = [
            jnp.where(low_half, y, 0.0),
            jnp.where(low_half, 0.0, turned),
            jnp.where(low_half, turned, 0.0),
            jnp.where(low_half, 0.0, y),
        ]
        block = jnp.concatenate(stack, axis=0).astype(BF16)
        out[s * 128 : (s + 1) * 128, :] = dot(right_z[...], block).astype(BF16)


def mix(received, weights, left_z, right_z):
    return call(
        mix_kernel,
        1,
        [whole((2048, 128)), whole((32, 128, 128)), whole((128, 128)), whole((128, 128))],
        [whole((2048, 128)), whole((512, 128))],
        [jax.ShapeDtypeStruct((2048, 128), BF16), jax.ShapeDtypeStruct((512, 128), BF16)],
        [pltpu.VMEM((512, 128), F32), pltpu.VMEM((512, 128), F32)],
        1 << 28,
        "mix_modes",
    )(received, weights, left_z, right_z)


def gelu_slope(v):
    k = 0.7978845608028654
    square = v * v
    t = jnp.tanh(v * (square * (k * 0.044715) + k))
    slope = v * (square * (3.0 * k * 0.044715) + k)
    return (1.0 + t) + (1.0 - t * t) * slope


def middle_kernel(received, local, cot, left_x, right_x, by_rows, by_blocks, out, planes, depth, first, messages):
    zq = pl.program_id(0)

    @pl.when(zq == 0)
    def _():
        planes[...] = received[...].astype(F32)

    for apg in range(4):
        rows = [
            planes[pl.ds((apg * 4 + j) * 8 + b2 * 4 + zq, 16, stride=128), :]
            for j in range(4)
            for b2 in range(2)
        ]
        turned = jnp.concatenate(rows, axis=0).T.astype(BF16)
        product = dot(turned, by_blocks[...])
        for j in range(4):
            depth[apg * 4 + j] = product[:, j * 128 : (j + 1) * 128].reshape(2, 2, 4, 8, 128)

    for group in range(4):
        block = jnp.concatenate(
            [depth[:, z2, :, group].reshape(256, 128).astype(BF16) for z2 in range(2)], axis=1
        )
        pre = dot(right_x[...], block)
        grads = []
        for z2 in range(2):
            rows = slice(group * 8, (group + 1) * 8)
            v = pre[:, z2 * 128 : (z2 + 1) * 128] + local[0, rows, z2].reshape(512, 128).astype(F32)
            c = 0.5 * cot[0, rows, z2].reshape(512, 128).astype(F32)
            grads.append((c * gelu_slope(v)).astype(BF16))
        store_x_modes(first, group, dot(left_x[...], jnp.concatenate(grads, axis=1)))
    y_modes_to_messages(first, by_rows[...], messages, zq)

    @pl.when(zq == 3)
    def _():
        out[...] = messages[...].astype(BF16)


def middle(received, local, cot, left_x, right_x, by_rows, by_blocks):
    plane = pl.BlockSpec((1, 32, 2, 64, 128), lambda i: (0, 0, i, 0, 0))
    return call(
        middle_kernel,
        4,
        [
            whole((2048, 128)),
            plane,
            plane,
            whole((256, 512)),
            whole((512, 256)),
            whole((32, 128)),
            whole((128, 512)),
        ],
        whole((2048, 128)),
        jax.ShapeDtypeStruct((2048, 128), BF16),
        [
            pltpu.VMEM((2048, 128), F32),
            pltpu.VMEM((16, 2, 2, 4, 8, 128), F32),
            pltpu.VMEM((16, 2, 2, 4, 8, 128), F32),
            pltpu.VMEM((2048, 128), F32),
        ],
        1 << 32,
        "gelu_gradient",
    )(received, local, cot, left_x, right_x, by_rows, by_blocks)


def update_kernel(received, kept, left_z, weight, moment, second, new_weight, new_moment, new_second, spectrum):
    step = pl.program_id(0)

    @pl.when(step == 0)
    def _():
        z_modes(received, left_z[...], spectrum)

    start = pl.multiple_of(step * 128, 128)
    left = kept[pl.ds(start, 128), :].astype(F32).T.astype(BF16)
    right = spectrum[pl.ds(start, 128), :].astype(BF16)
    zero = jnp.zeros((16, 128), BF16)
    columns = []
    for k in range(8):
        tiles = [zero] * 8
        tiles[k] = right[k * 16 : (k + 1) * 16]
        columns.append(jnp.concatenate(tiles, axis=0))
    product = dot(left, jnp.concatenate(columns, axis=1))
    for k in range(8):
        for b2 in range(2):
            for a2 in range(2):
                r = b2 * 2 + a2
                block = product[r * 32 : (r + 1) * 32, k * 128 : (k + 1) * 128]
                if r:
                    block = pltpu.roll(block, 128 - 32 * r, axis=1)
                grad = block[:, :32]
                w = weight[a2, b2, k]
                first = beta_one * moment[a2, b2, k] + (1.0 - beta_one) * grad
                square = beta_two * second[a2, b2, k] + (1.0 - beta_two) * grad * grad
                first_hat = first / (1.0 - beta_one**adam_step)
                second_hat = square / (1.0 - beta_two**adam_step)
                new_moment[a2, b2, k] = first
                new_second[a2, b2, k] = square
                new_weight[a2, b2, k] = w - learn_rate * (
                    first_hat / (jnp.sqrt(second_hat) + adam_eps) + decay_rate * w
                )


def update(received, kept, left_z, weight, moment, second):
    block = pl.BlockSpec((2, 2, 8, 32, 32), lambda i: (0, 0, i, 0, 0))
    return call(
        update_kernel,
        4,
        [whole((2048, 128)), whole((512, 128)), whole((128, 128)), block, block, block],
        [block] * 3,
        [jax.ShapeDtypeStruct(weight.shape, F32)] * 3,
        [pltpu.VMEM((512, 128), F32)],
        1 << 28,
        "adam_update",
    )(received, kept, left_z, weight, moment, second)


def exchange(messages):
    return lax.all_to_all(messages, ("dp", "mp"), split_axis=0, concat_axis=0, tiled=True)


def body(field, cotangent, spectral_weight, first_moment, second_moment, local_weight):
    left_x, right_x, by_rows, by_blocks, left_z, right_z = constants()
    eye = jnp.eye(8, dtype=BF16)
    left_c = (local_weight.T[:, None, :, None] * eye[None, :, None, :]).reshape(256, 256)
    received = exchange(forward(field, left_x, by_rows))
    local = local_mix(field, left_c)
    spread = spread_weights(spectral_weight)
    mixed, kept = mix(received, spread, left_z, right_z)
    received = exchange(mixed)
    received = exchange(middle(received, local, cotangent, left_x, right_x, by_rows, by_blocks))
    return tuple(update(received, kept, left_z, spectral_weight, first_moment, second_moment))


def solution(mesh):
    spread = P("dp", None, "mp", None, None)
    modes = P("mp", "dp", None, None, None)
    return jax.shard_map(
        body,
        mesh=mesh,
        in_specs=(spread, spread, modes, modes, modes, P()),
        out_specs=(modes, modes, modes),
        check_vma=False,
    )
```

time: 738 us -> 121 us (0.16); the launches traced: 729 us -> 120 us
  waiting for transfers between devices: 541 us -> 27.7 us
  matrix products: 48.3 us -> 0 us
  other arithmetic: 33.1 us -> 1.54 us
  Pallas kernels: 0 us -> 24 us
  local copies, waits for them, and re-layouts: 34.6 us -> 18.2 us
  between operations: 15.3 us -> 0.77 us
    unnamed x3 -> x0, waiting for transfers between devices: 377 us -> none
    all_gather x1 -> x0, waiting for transfers between devices: 145 us -> none  [body(): lax.all_gather(lowest_mode_weight, 'dp', axis=1, tiled=True)]
    dot_general x8 -> x0, matrix products: 48.3 us -> none  [the longest x1 19 us: project_onto_modes(): jnp.einsum('sczxy,yb->sczxb', block, cosine_sine_y_table, preferred_eleme...]
    pallas_call x0 -> x6, Pallas kernels: none -> 24 us  [the longest x1 9.63 us: middle(): call(middle_kernel, 4, [whole((2048, 128)), plane, plane, whole((256, 512...]
    convert_element_type x2 -> x1, other arithmetic: 13.9 us -> 0.01 us  [body(): eye = jnp.eye(8, dtype=BF16)]
    unnamed x1 -> x0, other arithmetic: 12.8 us -> none
    all_to_all x2, waiting for transfers between devices: 17.9 us -> 27.7 us  [exchange(): lax.all_to_all(messages, ('dp', 'mp'), split_axis=0, concat_axis=0, tiled...]
    convert_element_type x3 -> x0, local copies, waits for them, and re-layouts: 7.78 us -> none  [the longest x1 4.56 us: from_modes(): depth = jnp.einsum('scabk,zk->sczab', coeffs, cosine_sine_z_table, prefer...]
  transfers between devices with their start and end apart: 4 -> 2, of which waited for: 4 -> 2; matrix products, arithmetic and copies ran while one was open for 4% -> 5% of each run, Pallas kernels for 0% -> 3%
where the time goes in v1:
time: 121 us; the launch traced here: 120 us
  waiting for transfers between devices  27.7 us (23%)
  blocking collectives  25.8 us (21%)
  Pallas kernels  24 us (20%)
  starting transfers between devices  21.8 us (18%)
  local copies, waits for them, and re-layouts  18.2 us (15%)
  other arithmetic  1.54 us (1%)
    all_to_all x2, waiting for transfers between devices, exchange(): lax.all_to_all(messages, ('dp', 'mp'), split_axis=0, concat_axis=0, tiled...  27.7 us
    all_to_all x1, blocking collectives, exchange(): lax.all_to_all(messages, ('dp', 'mp'), split_axis=0, concat_axis=0, tiled...  25.8 us
    all_to_all x2, starting transfers between devices, exchange(): lax.all_to_all(messages, ('dp', 'mp'), split_axis=0, concat_axis=0, tiled...  21.8 us
    unnamed x36, local copies, waits for them, and re-layouts  14.1 us
    pallas_call x1, Pallas kernels, middle(): call(middle_kernel, 4, [whole((2048, 128)), plane, plane, whole((256, 512...  9.63 us
    pallas_call x1, Pallas kernels, update(): call(update_kernel, 4, [whole((2048, 128)), whole((512, 128)), whole((128...  4.83 us
    mul x1, local copies, waits for them, and re-layouts, body(): local_weight.T[:, None, :, None] * eye[None, :, None, :]  4.05 us
    pallas_call x1, Pallas kernels, forward(): call(forward_kernel, 4, [pl.BlockSpec((1, 32, 2, 64, 128), lambda i: (0,...  3.98 us
  transfers between devices with their start and end apart: 2, of which 2 were waited for; matrix products, arithmetic and copies ran while one was open for 5% of the time, Pallas kernels for 3%

profile of v1, /device:TPU:1, one launch (start us, length us, event | category | flops | bytes accessed | tf_op | source)
XLA Modules:
  0.0 119.9 jit_solution(10830259796423019473)
XLA Ops:
  0.6 0.0 copy-start.1
  0.6 2.2 %copy-done.1 = bf16[1,32,8,64,128]{4,3,2,1,0:T(8,128)(2,1)S(1)} copy-done((bf16[1,32,8,64,128]{4,3,2,1,0:T(8,128)(2,1)S(1)}, bf16[1,32,8,64,128]{4,3,2,1,0:T(8,128)(2,1)}, u32[]{:S(2)}) %copy-start.1) | copy-done | bytes 4194328
  2.8 0.0 copy-start.11
  2.8 0.9 copy-done.11
  3.8 0.0 copy-start.15
  3.8 0.7 copy-done.15
  4.5 0.0 copy-start
  4.5 4.0 %planes_to_modes.1 = bf16[2048,128]{1,0:T(8,128)(2,1)} custom-call(bf16[1,32,8,64,128]{4,3,2,1,0:T(8,128)(2,1)S(1)} %copy-done.1, bf16[256,512]{1,0:T(8,128)(2,1)S(1)} %copy-done.11, bf16[32,128]{1,0:T(8,128)(2,1)S(1)} %copy-done.15), custom_call_target="tpu_custom_call" | custom-call | flops 2147483648 | bytes 8388608 | tf_op jit(solution)/shard_map/planes_to_modes/pallas_call | solution.py:101
  8.4 0.0 copy-start.8
  8.5 0.0 copy-start.9
  8.5 16.7 %all-to-all-start = ((bf16[256,8,128]{2,1,0:T(8,128)(2,1)}), bf16[256,8,128]{2,1,0:T(8,128)(2,1)}, u32[]{:S(2)}, u32[]{:S(2)}) async-start(bf16[256,8,128]{2,1,0:T(8,128)(2,1)} %bitcast), calls=%async_computation | async-start | bytes 1048576 | tf_op jit(solution)/shard_map/all_to_all | solution.py:337
  25.1 0.0 copy-done
  25.1 1.0 spread_weights.1.weights
  26.2 0.0 copy-start.17
  26.2 19.1 %all-to-all-done = bf16[256,8,128]{2,1,0:T(8,128)(2,1)} async-done(((bf16[256,8,128]{2,1,0:T(8,128)(2,1)}), bf16[256,8,128]{2,1,0:T(8,128)(2,1)}, u32[]{:S(2)}, u32[]{:S(2)}) %all-to-all-start) | async-done | bytes 524320 | tf_op jit(solution)/shard_map/all_to_all | solution.py:337
  45.3 0.0 copy-done.8
  45.3 0.0 copy-done.9
  45.3 2.2 %mix_modes.1 = (bf16[2048,128]{1,0:T(8,128)(2,1)S(1)}, bf16[512,128]{1,0:T(8,128)(2,1)S(1)}) custom-call(bf16[2048,128]{1,0:T(8,128)(2,1)} %bitcast.1.received, bf16[32,128,128]{2,1,0:T(8,128)(2,1)S(1)} %spread_weights.1.weights, bf16[128,128]{1,0:T(8,128)(2,1)S(1)} %copy-done.8, bf16[128,128]{1,0:T(8,128)(2,1)S(1)} %copy-done.9), custom_call_target="tpu_custom_call" | custom-call | flops 268435456 | bytes 8388608 | tf_op jit(solution)/shard_map/mix_modes/pallas_call | solution.py:201
  47.4 0.0 copy-start.7
  47.4 0.8 copy-done.7
  48.2 5.2 %all-to-all-start.1 = ((bf16[256,8,128]{2,1,0:T(8,128)(2,1)}), bf16[256,8,128]{2,1,0:T(8,128)(2,1)S(1)}, u32[]{:S(2)}, u32[]{:S(2)}) async-start(bf16[256,8,128]{2,1,0:T(8,128)(2,1)} %bitcast.11), calls=%async_computation.1 | async-start | bytes 1048576 | tf_op jit(solution)/shard_map/all_to_all | solution.py:337
  53.4 0.0 copy-done.17
  53.4 0.1 copy.16
  53.5 1.5 %broadcast_multiply_fusion = bf16[32,8,32,8]{3,2,1,0:T(8,128)(2,1)} fusion(bf16[8,8]{1,0:T(8,128)(2,1)S(1)} %fusion, bf16[32,32]{1,0:T(8,128)(2,1)S(1)} %copy.16), kind=kLoop, calls=%fused_computation | loop fusion | flops 65536 | bytes 133248 | tf_op jit(solution)/shard_map/mul | solution.py:343
  55.0 4.1 %mul.20.left_c = bf16[256,256]{1,0:T(8,128)(2,1)S(1)} reshape(bf16[32,8,32,8]{3,2,1,0:T(8,128)(2,1)} %broadcast_multiply_fusion) | data formatting | bytes 262144 | tf_op jit(solution)/shard_map/mul | solution.py:343
  59.1 0.0 copy-start.2
  59.1 2.2 %copy-done.2 = bf16[1,32,8,64,128]{4,3,2,1,0:T(8,128)(2,1)S(1)} copy-done((bf16[1,32,8,64,128]{4,3,2,1,0:T(8,128)(2,1)S(1)}, bf16[1,32,8,64,128]{4,3,2,1,0:T(8,128)(2,1)}, u32[]{:S(2)}) %copy-start.2) | copy-done | bytes 4194328
  61.3 0.0 copy-start.12
  61.3 0.0 copy-start.14
  61.3 0.0 copy-start.16
  61.3 2.4 %local_mix.1.local = bf16[1,32,8,64,128]{4,3,2,1,0:T(8,128)(2,1)S(1)} custom-call(bf16[1,32,8,64,128]{4,3,2,1,0:T(8,128)(2,1)S(1)} %copy-done.2, bf16[256,256]{1,0:T(8,128)(2,1)S(1)} %mul.20.left_c), custom_call_target="tpu_custom_call" | custom-call | flops 2147483648 | bytes 8388608 | tf_op jit(solution)/shard_map/local_mix/pallas_call | solution.py:135
  63.7 0.0 copy-start.3
  63.7 1.9 %copy-done.3 = bf16[1,32,8,64,128]{4,3,2,1,0:T(8,128)(2,1)} copy-done((bf16[1,32,8,64,128]{4,3,2,1,0:T(8,128)(2,1)}, bf16[1,32,8,64,128]{4,3,2,1,0:T(8,128)(2,1)S(1)}, u32[]{:S(2)}) %copy-start.3) | copy-done | bytes 4194328
  65.6 8.6 %all-to-all-done.1 = bf16[256,8,128]{2,1,0:T(8,128)(2,1)S(1)} async-done(((bf16[256,8,128]{2,1,0:T(8,128)(2,1)}), bf16[256,8,128]{2,1,0:T(8,128)(2,1)S(1)}, u32[]{:S(2)}, u32[]{:S(2)}) %all-to-all-start.1) | async-done | bytes 524320 | tf_op jit(solution)/shard_map/all_to_all | solution.py:337
  74.3 0.0 copy-done.12
  74.3 0.0 copy-done.14
  74.3 0.0 copy-done.16
  74.3 0.0 copy-start.4
  74.3 2.2 %copy-done.4 = bf16[1,32,8,64,128]{4,3,2,1,0:T(8,128)(2,1)S(1)} copy-done((bf16[1,32,8,64,128]{4,3,2,1,0:T(8,128)(2,1)S(1)}, bf16[1,32,8,64,128]{4,3,2,1,0:T(8,128)(2,1)}, u32[]{:S(2)}) %copy-start.4) | copy-done | bytes 4194328
  76.5 0.0 copy-start.10
  76.5 2.2 %copy-done.10 = bf16[1,32,8,64,128]{4,3,2,1,0:T(8,128)(2,1)S(1)} copy-done((bf16[1,32,8,64,128]{4,3,2,1,0:T(8,128)(2,1)S(1)}, bf16[1,32,8,64,128]{4,3,2,1,0:T(8,128)(2,1)}, u32[]{:S(2)}) %copy-start.10) | copy-done | bytes 4194328
  78.6 0.0 copy-start.13
  78.6 0.9 copy-done.13
  79.6 0.0 copy-start.5
  79.6 0.0 copy-start.6
  79.6 9.6 %gelu_gradient.1 = bf16[2048,128]{1,0:T(8,128)(2,1)S(1)} custom-call(bf16[2048,128]{1,0:T(8,128)(2,1)S(1)} %bitcast.10, bf16[1,32,8,64,128]{4,3,2,1,0:T(8,128)(2,1)S(1)} %copy-done.4, bf16[1,32,8,64,128]{4,3,2,1,0:T(8,128)(2,1)S(1)} %copy-done.10, bf16[256,512]{1,0:T(8,128)(2,1)S(1)} %copy-done.12, bf16[512,256]{1,0:T(8,128)(2,1)S(1)} %copy-done.13, ...), custom_call_target="tpu_custom_call" | custom-call | flops 4294967296 | bytes 8388608 | tf_op jit(solution)/shard_map/gelu_gradient/pallas_call | solution.py:260
  89.2 25.8 %all_to_all.33 = bf16[256,8,128]{2,1,0:T(8,128)(2,1)S(1)} all-to-all(bf16[256,8,128]{2,1,0:T(8,128)(2,1)S(1)} %bitcast.12), channel_id=1, replica_groups=mesh['dp'=16,'mp'=16] {'dp','mp'}, dimensions={0} | all-to-all | bytes 1048576 | tf_op jit(solution)/shard_map/all_to_all | solution.py:337
  115.1 0.0 copy-done.5
  115.1 0.0 copy-done.6
  115.1 4.8 %adam_update.1 = (f32[2,2,32,32,32]{4,3,2,1,0:T(8,128)}, f32[2,2,32,32,32]{4,3,2,1,0:T(8,128)}, f32[2,2,32,32,32]{4,3,2,1,0:T(8,128)}) custom-call(bf16[2048,128]{1,0:T(8,128)(2,1)S(1)} %bitcast.9, bf16[512,128]{1,0:T(8,128)(2,1)S(1)} %get-tuple-element.6.kept, bf16[128,128]{1,0:T(8,128)(2,1)S(1)} %copy-done.8, f32[2,2,32,32,32]{4,3,2,1,0:T(8,128)S(1)} %copy-done, ...), custom_call_target="tpu_custom_call" | custom-call | flops 268435456 | bytes 8388608 | tf_op jit(solution)/shard_map/adam_update/pallas_call | solution.py:324
  (1 shorter events, 0.0 us)
Async XLA Ops:
  0.6 2.2 %copy-start.1 = (bf16[1,32,8,64,128]{4,3,2,1,0:T(8,128)(2,1)S(1)}, bf16[1,32,8,64,128]{4,3,2,1,0:T(8,128)(2,1)}, u32[]{:S(2)}) copy-start(bf16[1,32,8,64,128]{4,3,2,1,0:T(8,128)(2,1)} %field.3) | copy-start | bytes 12582916
  2.8 0.9 copy-start.11
  3.8 0.7 copy-start.15
  4.5 20.6 %copy-start = (f32[2,2,32,32,32]{4,3,2,1,0:T(8,128)S(1)}, f32[2,2,32,32,32]{4,3,2,1,0:T(8,128)}, u32[]{:S(2)}) copy-start(f32[2,2,32,32,32]{4,3,2,1,0:T(8,128)} %weight.3) | copy-start | bytes 1572868
  8.4 36.8 %copy-start.8 = (bf16[128,128]{1,0:T(8,128)(2,1)S(1)}, bf16[128,128]{1,0:T(8,128)(2,1)}, u32[]{:S(2)}) copy-start(bf16[128,128]{1,0:T(8,128)(2,1)} %constant.16.clone.left_z) | copy-start | bytes 98308
  8.5 36.8 %copy-start.9 = (bf16[128,128]{1,0:T(8,128)(2,1)S(1)}, bf16[128,128]{1,0:T(8,128)(2,1)}, u32[]{:S(2)}) copy-start(bf16[128,128]{1,0:T(8,128)(2,1)} %constant.17.clone.right_z) | copy-start | bytes 98308
  8.5 36.8 %all-to-all-start = ((bf16[256,8,128]{2,1,0:T(8,128)(2,1)}), bf16[256,8,128]{2,1,0:T(8,128)(2,1)}, u32[]{:S(2)}, u32[]{:S(2)}) async-start(bf16[256,8,128]{2,1,0:T(8,128)(2,1)} %bitcast), calls=%async_computation | async-start | bytes 1048576 | tf_op jit(solution)/shard_map/all_to_all | solution.py:337
  26.2 27.2 %copy-start.17 = (bf16[32,32]{1,0:T(8,128)(2,1)S(1)}, bf16[32,32]{1,0:T(8,128)(2,1)}, u32[]{:S(2)}) copy-start(bf16[32,32]{1,0:T(8,128)(2,1)} %param.17) | copy-start | bytes 6148
  47.4 0.8 copy-start.7
  48.2 26.0 %all-to-all-start.1 = ((bf16[256,8,128]{2,1,0:T(8,128)(2,1)}), bf16[256,8,128]{2,1,0:T(8,128)(2,1)S(1)}, u32[]{:S(2)}, u32[]{:S(2)}) async-start(bf16[256,8,128]{2,1,0:T(8,128)(2,1)} %bitcast.11), calls=%async_computation.1 | async-start | bytes 1048576 | tf_op jit(solution)/shard_map/all_to_all | solution.py:337
  59.1 2.2 %copy-start.2 = (bf16[1,32,8,64,128]{4,3,2,1,0:T(8,128)(2,1)S(1)}, bf16[1,32,8,64,128]{4,3,2,1,0:T(8,128)(2,1)}, u32[]{:S(2)}) copy-start(bf16[1,32,8,64,128]{4,3,2,1,0:T(8,128)(2,1)} %field.3) | copy-start | bytes 12582916
  61.3 13.0 %copy-start.12 = (bf16[256,512]{1,0:T(8,128)(2,1)S(1)}, bf16[256,512]{1,0:T(8,128)(2,1)}, u32[]{:S(2)}) copy-start(bf16[256,512]{1,0:T(8,128)(2,1)} %constant.12.clone.left_x) | copy-start | bytes 786436
  61.3 13.0 %copy-start.14 = (bf16[128,512]{1,0:T(8,128)(2,1)S(1)}, bf16[128,512]{1,0:T(8,128)(2,1)}, u32[]{:S(2)}) copy-start(bf16[128,512]{1,0:T(8,128)(2,1)} %constant.15.clone.by_blocks) | copy-start | bytes 393220
  61.3 13.0 %copy-start.16 = (bf16[32,128]{1,0:T(8,128)(2,1)S(1)}, bf16[32,128]{1,0:T(8,128)(2,1)}, u32[]{:S(2)}) copy-start(bf16[32,128]{1,0:T(8,128)(2,1)} %constant.14.clone.by_rows) | copy-start | bytes 24580
  63.7 1.9 %copy-start.3 = (bf16[1,32,8,64,128]{4,3,2,1,0:T(8,128)(2,1)}, bf16[1,32,8,64,128]{4,3,2,1,0:T(8,128)(2,1)S(1)}, u32[]{:S(2)}) copy-start(bf16[1,32,8,64,128]{4,3,2,1,0:T(8,128)(2,1)S(1)} %local_mix.1.local) | copy-start | bytes 12582916
  74.3 2.2 %copy-start.4 = (bf16[1,32,8,64,128]{4,3,2,1,0:T(8,128)(2,1)S(1)}, bf16[1,32,8,64,128]{4,3,2,1,0:T(8,128)(2,1)}, u32[]{:S(2)}) copy-start(bf16[1,32,8,64,128]{4,3,2,1,0:T(8,128)(2,1)} %copy-done.3) | copy-start | bytes 12582916
  76.5 2.2 %copy-start.10 = (bf16[1,32,8,64,128]{4,3,2,1,0:T(8,128)(2,1)S(1)}, bf16[1,32,8,64,128]{4,3,2,1,0:T(8,128)(2,1)}, u32[]{:S(2)}) copy-start(bf16[1,32,8,64,128]{4,3,2,1,0:T(8,128)(2,1)} %cot.1) | copy-start | bytes 12582916
  78.6 0.9 copy-start.13
  79.6 35.5 %copy-start.5 = (f32[2,2,32,32,32]{4,3,2,1,0:T(8,128)S(1)}, f32[2,2,32,32,32]{4,3,2,1,0:T(8,128)}, u32[]{:S(2)}) copy-start(f32[2,2,32,32,32]{4,3,2,1,0:T(8,128)} %moment.1) | copy-start | bytes 1572868
  79.6 35.5 %copy-start.6 = (f32[2,2,32,32,32]{4,3,2,1,0:T(8,128)S(1)}, f32[2,2,32,32,32]{4,3,2,1,0:T(8,128)}, u32[]{:S(2)}) copy-start(f32[2,2,32,32,32]{4,3,2,1,0:T(8,128)} %second.1) | copy-start | bytes 1572868

commit v2 on v1

v2 whole, which is shorter than its diff:
```python
import jax
import jax.numpy as jnp
import ml_dtypes
import numpy as np
from jax import lax
from jax.experimental import pallas as pl
from jax.experimental.pallas import tpu as pltpu
from jax.sharding import PartitionSpec as P

beta_one = 0.9
beta_two = 0.999
learn_rate = 0.001
decay_rate = 0.1
adam_eps = 1e-08
adam_step = 1000.0

F32 = jnp.float32
BF16 = jnp.bfloat16
MIB = 1024 * 1024


def table(length, modes=16):
    grid = np.arange(length, dtype=np.float32)[:, None]
    index = np.arange(2 * modes, dtype=np.float32)[None, :]
    freq = np.where(index < modes, index, index - np.float32(modes - 1)).astype(np.float32)
    phase = (np.float32(2.0 * np.pi) * freq * grid / np.float32(length)).astype(np.float32)
    values = np.where(index < modes, np.cos(phase), np.sin(phase)) * np.sqrt(np.float32(2.0 / length))
    return values.astype(np.float32).astype(ml_dtypes.bfloat16).astype(np.float32)


def constants():
    bx, by, bz = table(64), table(128), table(128)
    left_x = np.einsum("xa,cd->acdx", bx, np.eye(4)).reshape(128, 256)
    right_x = np.einsum("xpt,cd,gh->gcxphtd", bx.reshape(64, 16, 2), np.eye(4), np.eye(2)).reshape(512, 256)
    right_y = np.einsum("yb,qr->qybr", by, np.eye(4)).reshape(512, 128)
    left_z = np.einsum("nqtk,bd->btkndq", bz.reshape(16, 4, 2, 32), np.eye(2)).reshape(128, 128)
    order = np.eye(128).reshape(2, 2, 8, 4, 128).transpose(0, 2, 1, 3, 4).reshape(128, 128).T
    low = lambda v: jnp.asarray(np.ascontiguousarray(v).astype(ml_dtypes.bfloat16))
    left_y = right_y.T
    tables = (left_x, right_x, left_y, left_y * 0.5, left_z, left_z.T, order, order.T)
    return [low(v) for v in tables]


def dot(a, b):
    return lax.dot_general(a, b, (((1,), (0,)), ((), ())), preferred_element_type=F32)


def dot_nt(a, b):
    return lax.dot_general(a, b, (((1,), (1,)), ((), ())), preferred_element_type=F32)


def whole(shape):
    zeros = (0,) * len(shape)
    return pl.BlockSpec(shape, lambda i: zeros)


def resident():
    return pl.BlockSpec(memory_space=pltpu.VMEM)


def call(kernel, grid, in_specs, out_specs, out_shape, scratch, flops, name, vmem):
    return pl.pallas_call(
        kernel,
        grid=(grid,),
        in_specs=in_specs,
        out_specs=out_specs,
        out_shape=out_shape,
        scratch_shapes=scratch,
        compiler_params=pltpu.CompilerParams(vmem_limit_bytes=vmem * MIB),
        cost_estimate=pl.CostEstimate(flops=flops, bytes_accessed=8 << 20, transcendentals=0),
        name=name,
    )


def store_x_modes(first, left_x, zq, group, planes):
    halves = []
    for half in range(2):
        rows = slice(half * 256, (half + 1) * 256)
        block = jnp.concatenate([p[rows] for p in planes], axis=1)
        halves.append(dot(left_x, block).reshape(16, 1, 8, 256))
    both = jnp.concatenate(halves, axis=1).reshape(16, 16, 256).astype(BF16)
    for z2 in range(2):
        first[:, zq, z2, group] = both[:, :, z2 * 128 : (z2 + 1) * 128]


def store_messages(first, left_y, out):
    for pair in range(8):
        planes = [first[pair * 2 : pair * 2 + 2, zq].reshape(256, 128) for zq in range(4)]
        planar = dot_nt(left_y, jnp.concatenate(planes, axis=1))
        tiles = [planar[:, :128].reshape(16, 8, 128), planar[:, 128:].reshape(16, 8, 128)]
        out[:, pair] = jnp.concatenate(tiles, axis=1).astype(BF16)


def forward_kernel(field, left_x, left_y, out, first):
    zq = pl.program_id(0)
    for group in range(4):
        planes = [field[0, group * 8 : (group + 1) * 8, z2].reshape(512, 128) for z2 in range(2)]
        store_x_modes(first, left_x[...], zq, group, planes)

    @pl.when(zq == 3)
    def _():
        store_messages(first, left_y[...], out)


FIRST = (16, 4, 2, 4, 16, 128)
MESSAGES = (16, 8, 16, 128)


def forward(field, left_x, left_y):
    return call(
        forward_kernel,
        4,
        [
            pl.BlockSpec((1, 32, 2, 64, 128), lambda i: (0, 0, i, 0, 0)),
            whole((128, 256)),
            whole((128, 512)),
        ],
        whole(MESSAGES),
        jax.ShapeDtypeStruct(MESSAGES, BF16),
        [pltpu.VMEM(FIRST, BF16)],
        1 << 31,
        "planes_to_modes",
        60,
    )(field, left_x, left_y).reshape(2048, 128)


def local_kernel(field, left_c, out):
    for xg in range(4):
        cols = []
        for z2 in range(2):
            rows = field[0, :, z2, xg * 16 : (xg + 1) * 16, :].astype(F32)
            cols.append(rows.reshape(32, 2, 8, 128))
        halves = []
        for half in range(2):
            block = jnp.concatenate([c[:, half].reshape(256, 128) for c in cols], axis=1)
            halves.append(dot(left_c[...], block.astype(BF16)))
        for z2 in range(2):
            parts = [h[:, z2 * 128 : (z2 + 1) * 128].reshape(32, 1, 8, 128) for h in halves]
            both = jnp.concatenate(parts, axis=1).reshape(32, 16, 128)
            out[0, :, z2, xg * 16 : (xg + 1) * 16, :] = both.astype(BF16)


def local_mix(field, left_c):
    plane = pl.BlockSpec((1, 32, 2, 64, 128), lambda i: (0, 0, i, 0, 0))
    return call(
        local_kernel,
        4,
        [plane, whole((256, 256))],
        plane,
        jax.ShapeDtypeStruct(field.shape, BF16),
        [],
        1 << 31,
        "local_mix",
        24,
    )(field, left_c)


def spread_kernel(weight, order, order_t, out):
    rows = []
    for b2 in range(2):
        for a2 in range(2):
            r = b2 * 2 + a2
            flat = weight[a2, b2].reshape(256, 32).astype(BF16)
            rows.append(dot(flat, order[r * 32 : (r + 1) * 32, :]).astype(BF16))
    for k in range(8):
        block = jnp.concatenate([v[k * 32 : (k + 1) * 32] for v in rows], axis=0)
        out[k] = dot(order_t[...], block).astype(BF16)


def spread_weights(weight, order, order_t):
    return call(
        spread_kernel,
        4,
        [pl.BlockSpec((2, 2, 8, 32, 32), lambda i: (0, 0, i, 0, 0)), whole((128, 128)), whole((128, 128))],
        pl.BlockSpec((8, 128, 128), lambda i: (i, 0, 0)),
        jax.ShapeDtypeStruct((32, 128, 128), BF16),
        [],
        1 << 28,
        "spread_weights",
        16,
    )(weight, order, order_t)


def z_modes(received, left_z, spectrum):
    low_half = lax.broadcasted_iota(jnp.int32, (32, 128), 1) < 64
    for pair in range(8):
        both = [received[s * 128 : (s + 1) * 128, :] for s in (2 * pair, 2 * pair + 1)]
        product = dot(left_z, jnp.concatenate(both, axis=1))
        for odd in range(2):
            p = product[:, odd * 128 : (odd + 1) * 128]
            stay = jnp.where(low_half, p[0:32], p[96:128])
            move = jnp.where(low_half, p[64:96], p[32:64])
            spectrum[pl.ds(2 * pair + odd, 32, stride=16), :] = stay + pltpu.roll(move, 64, axis=1)


def mix_kernel(received, weights, left_z, right_z, out, kept, spectrum, mixed):
    z_modes(received, left_z[...], spectrum)
    kept[...] = spectrum[...].astype(BF16)
    for k in range(32):
        rows = slice(k * 16, (k + 1) * 16)
        mixed[rows, :] = dot(spectrum[rows, :].astype(BF16), weights[k])
    low_half = lax.broadcasted_iota(jnp.int32, (32, 128), 1) < 64
    for pair in range(8):
        blocks = []
        for s in (2 * pair, 2 * pair + 1):
            y = mixed[pl.ds(s, 32, stride=16), :]
            turned = pltpu.roll(y, 64, axis=1)
            stack = [
                jnp.where(low_half, y, 0.0),
                jnp.where(low_half, 0.0, turned),
                jnp.where(low_half, turned, 0.0),
                jnp.where(low_half, 0.0, y),
            ]
            blocks.append(jnp.concatenate(stack, axis=0).astype(BF16))
        product = dot(right_z[...], jnp.concatenate(blocks, axis=1)).astype(BF16)
        for odd in range(2):
            s = 2 * pair + odd
            out[s * 128 : (s + 1) * 128, :] = product[:, odd * 128 : (odd + 1) * 128]


def mix(received, weights, left_z, right_z):
    return call(
        mix_kernel,
        1,
        [whole((2048, 128)), whole((32, 128, 128)), whole((128, 128)), whole((128, 128))],
        [whole((2048, 128)), whole((512, 128))],
        [jax.ShapeDtypeStruct((2048, 128), BF16), jax.ShapeDtypeStruct((512, 128), BF16)],
        [pltpu.VMEM((512, 128), F32), pltpu.VMEM((512, 128), F32)],
        1 << 34,
        "mix_modes",
        16,
    )(received, weights, left_z, right_z)


def gelu_pull(v, cot):
    k = 0.7978845608028654
    square = v * v
    t = jnp.tanh(v * (square * low(k * 0.044715) + low(k)))
    slope = v * (square * low(3.0 * k * 0.044715) + low(k))
    one = low(1.0)
    return cot * ((one + t) * (one + (one - t) * slope))


def low(value):
    return jnp.asarray(value, BF16)


def middle_kernel(received, local, cot, left_x, right_x, left_y, half_y, out, depth, first, spectral):
    turned = []
    for pair in range(8):
        both = received[:, pair].astype(F32).reshape(16, 2, 8, 128)
        for odd in range(2):
            turned.append(both[:, odd].reshape(128, 128).T.astype(BF16))
    product = dot(jnp.concatenate(turned, axis=0), left_y[...]).astype(BF16)
    for zq in range(4):
        depth[zq] = product[:, zq * 128 : (zq + 1) * 128].reshape(16, 2, 4, 16, 128)

    def inverse(zq, group):
        block = jnp.concatenate([depth[zq, :, z2, group].reshape(256, 128) for z2 in range(2)], axis=1)
        spectral[group % 2] = dot(right_x[...], block).astype(BF16)

    def quarter(zq, carry):
        inverse(zq, 0)
        for group in range(4):
            if group < 3:
                inverse(zq, group + 1)
            planes = []
            for z2 in range(2):
                rows = slice(group * 8, (group + 1) * 8)
                v = spectral[group % 2, :, z2 * 128 : (z2 + 1) * 128]
                v = v + local[0, rows, zq * 2 + z2].reshape(512, 128)
                planes.append(gelu_pull(v, cot[0, rows, zq * 2 + z2].reshape(512, 128)))
            store_x_modes(first, left_x[...], zq, group, planes)
        return carry

    lax.fori_loop(0, 4, quarter, 0)
    store_messages(first, half_y[...], out)


def middle(received, local, cot, left_x, right_x, left_y, half_y):
    return call(
        middle_kernel,
        1,
        [
            whole(MESSAGES),
            resident(),
            resident(),
            whole((128, 256)),
            whole((512, 256)),
            whole((128, 512)),
            whole((128, 512)),
        ],
        whole(MESSAGES),
        jax.ShapeDtypeStruct(MESSAGES, BF16),
        [
            pltpu.VMEM((4, 16, 2, 4, 16, 128), BF16),
            pltpu.VMEM(FIRST, BF16),
            pltpu.VMEM((2, 512, 256), BF16),
        ],
        1 << 32,
        "gelu_gradient",
        32,
    )(received.reshape(MESSAGES), local, cot, left_x, right_x, left_y, half_y).reshape(2048, 128)


def update_kernel(received, kept, left_z, order_t, weight, moment, second, new_weight, new_moment, new_second, spectrum):
    step = pl.program_id(0)

    @pl.when(step == 0)
    def _():
        z_modes(received, left_z[...], spectrum)

    start = pl.multiple_of(step * 128, 128)
    left = dot(kept[pl.ds(start, 128), :], order_t[...]).T.astype(BF16)
    right = dot(spectrum[pl.ds(start, 128), :].astype(BF16), order_t[...]).astype(BF16)
    zero = jnp.zeros((16, 128), BF16)
    columns = []
    for k in range(8):
        tiles = [zero] * 8
        tiles[k] = right[k * 16 : (k + 1) * 16]
        columns.append(jnp.concatenate(tiles, axis=0))
    product = dot(left, jnp.concatenate(columns, axis=1))
    for k in range(8):
        for b2 in range(2):
            for a2 in range(2):
                r = b2 * 2 + a2
                block = product[r * 32 : (r + 1) * 32, k * 128 : (k + 1) * 128]
                if r:
                    block = pltpu.roll(block, 128 - 32 * r, axis=1)
                grad = block[:, :32]
                w = weight[a2, b2, step * 8 + k]
                first = beta_one * moment[a2, b2, step * 8 + k] + (1.0 - beta_one) * grad
                square = beta_two * second[a2, b2, step * 8 + k] + (1.0 - beta_two) * grad * grad
                first_hat = first / (1.0 - beta_one**adam_step)
                second_hat = square / (1.0 - beta_two**adam_step)
                new_moment[a2, b2, k] = first
                new_second[a2, b2, k] = square
                new_weight[a2, b2, k] = w - learn_rate * (
                    first_hat / (jnp.sqrt(second_hat) + adam_eps) + decay_rate * w
                )


def update(received, kept, left_z, order_t, weight, moment, second):
    block = pl.BlockSpec((2, 2, 8, 32, 32), lambda i: (0, 0, i, 0, 0))
    return call(
        update_kernel,
        4,
        [whole((2048, 128)), whole((512, 128)), whole((128, 128)), whole((128, 128)), resident(), resident(), resident()],
        [block] * 3,
        [jax.ShapeDtypeStruct(weight.shape, F32)] * 3,
        [pltpu.VMEM((512, 128), F32)],
        1 << 28,
        "adam_update",
        24,
    )(received, kept, left_z, order_t, weight, moment, second)


def exchange(messages):
    return lax.all_to_all(messages, ("dp", "mp"), split_axis=0, concat_axis=0, tiled=True)


def body(field, cotangent, spectral_weight, first_moment, second_moment, local_weight):
    left_x, right_x, left_y, half_y, left_z, right_z, order, order_t = constants()
    eye = jnp.eye(8, dtype=BF16)
    left_c = (local_weight.T[:, None, :, None] * eye[None, :, None, :]).reshape(256, 256)
    received = exchange(forward(field, left_x, left_y))
    local = local_mix(field, left_c)
    spread = spread_weights(spectral_weight, order, order_t)
    received, local, spread = lax.optimization_barrier((received, local, spread))
    mixed, kept = mix(received, spread, left_z, right_z)
    received = exchange(mixed)
    received = exchange(middle(received, local, cotangent, left_x, right_x, left_y, half_y))
    return tuple(update(received, kept, left_z, order_t, spectral_weight, first_moment, second_moment))


def solution(mesh):
    spread = P("dp", None, "mp", None, None)
    modes = P("mp", "dp", None, None, None)
    return jax.shard_map(
        body,
        mesh=mesh,
        in_specs=(spread, spread, modes, modes, modes, P()),
        out_specs=(modes, modes, modes),
        check_vma=False,
    )
```

time: 121 us -> 112 us (0.926)
  blocking collectives: 25.8 us -> 54.3 us
  waiting for transfers between devices: 27.7 us -> 6.14 us
  local copies, waits for them, and re-layouts: 18.2 us -> 8.35 us
  starting transfers between devices: 21.8 us -> 16.7 us
    all_to_all x1 -> x2, blocking collectives: 25.8 us -> 54.3 us  [exchange(): lax.all_to_all(messages, ('dp', 'mp'), split_axis=0, concat_axis=0, tiled...]
    all_to_all x2 -> x1, waiting for transfers between devices: 27.7 us -> 6.14 us  [exchange(): lax.all_to_all(messages, ('dp', 'mp'), split_axis=0, concat_axis=0, tiled...]
    unnamed x36 -> x32, local copies, waits for them, and re-layouts: 14.1 us -> 4.21 us
    all_to_all x2 -> x1, starting transfers between devices: 21.8 us -> 16.7 us  [exchange(): lax.all_to_all(messages, ('dp', 'mp'), split_axis=0, concat_axis=0, tiled...]
    pallas_call x1, Pallas kernels: 9.63 us -> 7.57 us  [middle(): call(middle_kernel, 1, [whole(MESSAGES), resident(), resident(), whole((1...]
  transfers between devices with their start and end apart: 2 -> 1, of which waited for: 2 -> 1; matrix products, arithmetic and copies ran while one was open for 5% -> 5% of each run, Pallas kernels for 3% -> 4%
where the time goes in v2:
time: 112 us
  blocking collectives  54.3 us (48%)
  Pallas kernels  24 us (21%)
  starting transfers between devices  16.7 us (15%)
  local copies, waits for them, and re-layouts  8.35 us (7%)
  waiting for transfers between devices  6.14 us (5%)
  other arithmetic  1.53 us (1%)
    all_to_all x2, blocking collectives, exchange(): lax.all_to_all(messages, ('dp', 'mp'), split_axis=0, concat_axis=0, tiled...  54.3 us
    all_to_all x1, starting transfers between devices, exchange(): lax.all_to_all(messages, ('dp', 'mp'), split_axis=0, concat_axis=0, tiled...  16.7 us
    pallas_call x1, Pallas kernels, middle(): call(middle_kernel, 1, [whole(MESSAGES), resident(), resident(), whole((1...  7.57 us
    all_to_all x1, waiting for transfers between devices, exchange(): lax.all_to_all(messages, ('dp', 'mp'), split_axis=0, concat_axis=0, tiled...  6.14 us
    pallas_call x1, Pallas kernels, forward(): call(forward_kernel, 4, [pl.BlockSpec((1, 32, 2, 64, 128), lambda i: (0,...  5.18 us
    pallas_call x1, Pallas kernels, update(): call(update_kernel, 4, [whole((2048, 128)), whole((512, 128)), whole((128...  4.86 us
    unnamed x32, local copies, waits for them, and re-layouts  4.21 us
    mul x1, local copies, waits for them, and re-layouts, body(): local_weight.T[:, None, :, None] * eye[None, :, None, :]  4.05 us
  transfers between devices with their start and end apart: 1, of which 1 were waited for; matrix products, arithmetic and copies ran while one was open for 5% of the time, Pallas kernels for 4%

profile of v2, /device:TPU:1, one launch (start us, length us, event | category | flops | bytes accessed | tf_op | source)
XLA Modules:
  0.0 111.8 jit_solution(7819294819405860178)
XLA Ops:
  0.6 0.0 copy-start.15
  0.6 5.2 %planes_to_modes.1 = bf16[16,8,16,128]{3,2,1,0:T(8,128)(2,1)} custom-call(bf16[1,32,8,64,128]{4,3,2,1,0:T(8,128)(2,1)} %field.3, bf16[128,256]{1,0:T(8,128)(2,1)} %constant.16.clone.left_x, bf16[128,512]{1,0:T(8,128)(2,1)} %constant.18.clone.left_y), custom_call_target="tpu_custom_call" | custom-call | flops 2147483648 | bytes 8388608 | tf_op jit(solution)/shard_map/planes_to_modes/pallas_call | solution.py:110
  5.8 16.7 %all-to-all-start = ((bf16[256,8,128]{2,1,0:T(8,128)(2,1)}), bf16[256,8,128]{2,1,0:T(8,128)(2,1)}, u32[]{:S(2)}, u32[]{:S(2)}) async-start(bf16[256,8,128]{2,1,0:T(8,128)(2,1)} %bitcast.13), calls=%async_computation | async-start | bytes 1048576 | tf_op jit(solution)/shard_map/all_to_all | solution.py:359
  22.5 0.0 copy-done.15
  22.5 0.1 copy.18
  22.6 0.0 copy-start
  22.6 0.0 copy-start.6
  22.6 0.0 copy-start.8
  22.6 1.5 %broadcast_multiply_fusion = bf16[32,8,32,8]{3,2,1,0:T(8,128)(2,1)} fusion(bf16[8,8]{1,0:T(8,128)(2,1)S(1)} %fusion, bf16[32,32]{1,0:T(8,128)(2,1)S(1)} %copy.18), kind=kLoop, calls=%fused_computation | loop fusion | flops 65536 | bytes 133248 | tf_op jit(solution)/shard_map/mul | solution.py:365
  24.2 4.1 %mul.20.left_c = bf16[256,256]{1,0:T(8,128)(2,1)S(1)} reshape(bf16[32,8,32,8]{3,2,1,0:T(8,128)(2,1)} %broadcast_multiply_fusion) | data formatting | bytes 262144 | tf_op jit(solution)/shard_map/mul | solution.py:365
  28.2 0.0 copy-done
  28.2 0.0 copy-done.6
  28.2 0.0 copy-done.8
  28.3 1.7 %spread_weights.1.weights = bf16[32,128,128]{2,1,0:T(8,128)(2,1)S(1)} custom-call(f32[2,2,32,32,32]{4,3,2,1,0:T(8,128)S(1)} %copy-done, bf16[128,128]{1,0:T(8,128)(2,1)S(1)} %copy-done.8, bf16[128,128]{1,0:T(8,128)(2,1)S(1)} %copy-done.6), custom_call_target="tpu_custom_call" | custom-call | flops 268435456 | bytes 8388608 | tf_op jit(solution)/shard_map/spread_weights/pallas_call | solution.py:171
  30.0 0.0 copy-start.1
  30.0 2.2 %copy-done.1 = bf16[1,32,8,64,128]{4,3,2,1,0:T(8,128)(2,1)S(1)} copy-done((bf16[1,32,8,64,128]{4,3,2,1,0:T(8,128)(2,1)S(1)}, bf16[1,32,8,64,128]{4,3,2,1,0:T(8,128)(2,1)}, u32[]{:S(2)}) %copy-start.1) | copy-done | bytes 4194328
  32.2 0.0 copy-start.7
  32.2 0.0 copy-start.14
  32.2 2.3 %local_mix.1.local = bf16[1,32,8,64,128]{4,3,2,1,0:T(8,128)(2,1)S(1)} custom-call(bf16[1,32,8,64,128]{4,3,2,1,0:T(8,128)(2,1)S(1)} %copy-done.1, bf16[256,256]{1,0:T(8,128)(2,1)S(1)} %mul.20.left_c), custom_call_target="tpu_custom_call" | custom-call | flops 2147483648 | bytes 8388608 | tf_op jit(solution)/shard_map/local_mix/pallas_call | solution.py:145
  34.5 0.0 copy-start.2
  34.5 1.9 %copy-done.2 = bf16[1,32,8,64,128]{4,3,2,1,0:T(8,128)(2,1)} copy-done((bf16[1,32,8,64,128]{4,3,2,1,0:T(8,128)(2,1)}, bf16[1,32,8,64,128]{4,3,2,1,0:T(8,128)(2,1)S(1)}, u32[]{:S(2)}) %copy-start.2) | copy-done | bytes 4194328
  36.5 6.1 %all-to-all-done = bf16[256,8,128]{2,1,0:T(8,128)(2,1)} async-done(((bf16[256,8,128]{2,1,0:T(8,128)(2,1)}), bf16[256,8,128]{2,1,0:T(8,128)(2,1)}, u32[]{:S(2)}, u32[]{:S(2)}) %all-to-all-start) | async-done | bytes 524320 | tf_op jit(solution)/shard_map/all_to_all | solution.py:359
  42.6 0.0 copy-done.7
  42.6 0.0 copy-done.14
  42.6 0.0 copy-start.3
  42.6 0.0 copy-start.9
  42.7 0.0 copy-start.10
  42.7 0.0 copy-start.11
  42.7 0.0 copy-start.12
  42.7 0.0 copy-start.13
  42.7 2.3 %mix_modes.1 = (bf16[2048,128]{1,0:T(8,128)(2,1)S(1)}, bf16[512,128]{1,0:T(8,128)(2,1)S(1)}) custom-call(bf16[2048,128]{1,0:T(8,128)(2,1)} %bitcast.1.received, bf16[32,128,128]{2,1,0:T(8,128)(2,1)S(1)} %spread_weights.1.weights, bf16[128,128]{1,0:T(8,128)(2,1)S(1)} %copy-done.7, bf16[128,128]{1,0:T(8,128)(2,1)S(1)} %copy-done.14), custom_call_target="tpu_custom_call" | custom-call | flops 17179869184 | bytes 8388608 | tf_op jit(solution)/shard_map/mix_modes/pallas_call | solution.py:222
  45.0 28.4 %all_to_all.32 = bf16[256,8,128]{2,1,0:T(8,128)(2,1)S(1)} all-to-all(bf16[256,8,128]{2,1,0:T(8,128)(2,1)S(1)} %bitcast.12), channel_id=1, replica_groups=mesh['dp'=16,'mp'=16] {'dp','mp'}, dimensions={0} | all-to-all | bytes 1048576 | tf_op jit(solution)/shard_map/all_to_all | solution.py:359
  73.4 0.0 copy-done.3
  73.4 0.0 copy-done.9
  73.4 0.0 copy-done.10
  73.4 0.0 copy-done.11
  73.5 0.0 copy-done.12
  73.5 0.0 copy-done.13
  73.5 0.0 copy-start.4
  73.5 0.0 copy-start.5
  73.5 7.6 %gelu_gradient.1 = bf16[16,8,16,128]{3,2,1,0:T(8,128)(2,1)S(1)} custom-call(bf16[16,8,16,128]{3,2,1,0:T(8,128)(2,1)S(1)} %bitcast.10, bf16[1,32,8,64,128]{4,3,2,1,0:T(8,128)(2,1)S(1)} %copy-done.3, bf16[1,32,8,64,128]{4,3,2,1,0:T(8,128)(2,1)S(1)} %copy-done.9, bf16[128,256]{1,0:T(8,128)(2,1)S(1)} %copy-done.13, bf16[512,256]{1,0:T(8,128)(2,1)S(1)} %copy-done.10, ...), custom_call_target="tpu_custom_call" | custom-call | flops 4294967296 | bytes 8388608 | tf_op jit(solution)/shard_map/gelu_gradient/pallas_call | solution.py:281
  81.1 25.8 %all_to_all.33 = bf16[256,8,128]{2,1,0:T(8,128)(2,1)S(1)} all-to-all(bf16[256,8,128]{2,1,0:T(8,128)(2,1)S(1)} %bitcast.11), channel_id=1, replica_groups=mesh['dp'=16,'mp'=16] {'dp','mp'}, dimensions={0} | all-to-all | bytes 1048576 | tf_op jit(solution)/shard_map/all_to_all | solution.py:359
  106.9 0.0 copy-done.4
  106.9 0.0 copy-done.5
  106.9 4.9 %adam_update.1 = (f32[2,2,32,32,32]{4,3,2,1,0:T(8,128)}, f32[2,2,32,32,32]{4,3,2,1,0:T(8,128)}, f32[2,2,32,32,32]{4,3,2,1,0:T(8,128)}) custom-call(bf16[2048,128]{1,0:T(8,128)(2,1)S(1)} %bitcast.9, bf16[512,128]{1,0:T(8,128)(2,1)S(1)} %get-tuple-element.12.kept, bf16[128,128]{1,0:T(8,128)(2,1)S(1)} %copy-done.7, bf16[128,128]{1,0:T(8,128)(2,1)S(1)} %copy-done.6, ...), custom_call_target="tpu_custom_call" | custom-call | flops 268435456 | bytes 8388608 | tf_op jit(solution)/shard_map/adam_update/pallas_call | solution.py:345
  (1 shorter events, 0.0 us)
Async XLA Ops:
  0.6 21.9 %copy-start.15 = (bf16[32,32]{1,0:T(8,128)(2,1)S(1)}, bf16[32,32]{1,0:T(8,128)(2,1)}, u32[]{:S(2)}) copy-start(bf16[32,32]{1,0:T(8,128)(2,1)} %param.19) | copy-start | bytes 6148
  5.8 36.8 %all-to-all-start = ((bf16[256,8,128]{2,1,0:T(8,128)(2,1)}), bf16[256,8,128]{2,1,0:T(8,128)(2,1)}, u32[]{:S(2)}, u32[]{:S(2)}) async-start(bf16[256,8,128]{2,1,0:T(8,128)(2,1)} %bitcast.13), calls=%async_computation | async-start | bytes 1048576 | tf_op jit(solution)/shard_map/all_to_all | solution.py:359
  22.6 5.6 %copy-start = (f32[2,2,32,32,32]{4,3,2,1,0:T(8,128)S(1)}, f32[2,2,32,32,32]{4,3,2,1,0:T(8,128)}, u32[]{:S(2)}) copy-start(f32[2,2,32,32,32]{4,3,2,1,0:T(8,128)} %weight.3) | copy-start | bytes 1572868
  22.6 5.6 %copy-start.6 = (bf16[128,128]{1,0:T(8,128)(2,1)S(1)}, bf16[128,128]{1,0:T(8,128)(2,1)}, u32[]{:S(2)}) copy-start(bf16[128,128]{1,0:T(8,128)(2,1)} %constant.23.clone.order_t) | copy-start | bytes 98308
  22.6 5.6 %copy-start.8 = (bf16[128,128]{1,0:T(8,128)(2,1)S(1)}, bf16[128,128]{1,0:T(8,128)(2,1)}, u32[]{:S(2)}) copy-start(bf16[128,128]{1,0:T(8,128)(2,1)} %constant.22.clone.order) | copy-start | bytes 98308
  30.0 2.2 %copy-start.1 = (bf16[1,32,8,64,128]{4,3,2,1,0:T(8,128)(2,1)S(1)}, bf16[1,32,8,64,128]{4,3,2,1,0:T(8,128)(2,1)}, u32[]{:S(2)}) copy-start(bf16[1,32,8,64,128]{4,3,2,1,0:T(8,128)(2,1)} %field.3) | copy-start | bytes 12582916
  32.2 10.4 %copy-start.7 = (bf16[128,128]{1,0:T(8,128)(2,1)S(1)}, bf16[128,128]{1,0:T(8,128)(2,1)}, u32[]{:S(2)}) copy-start(bf16[128,128]{1,0:T(8,128)(2,1)} %constant.20.clone.left_z) | copy-start | bytes 98308
  32.2 10.4 %copy-start.14 = (bf16[128,128]{1,0:T(8,128)(2,1)S(1)}, bf16[128,128]{1,0:T(8,128)(2,1)}, u32[]{:S(2)}) copy-start(bf16[128,128]{1,0:T(8,128)(2,1)} %constant.21.clone.right_z) | copy-start | bytes 98308
  34.5 2.0 %copy-start.2 = (bf16[1,32,8,64,128]{4,3,2,1,0:T(8,128)(2,1)}, bf16[1,32,8,64,128]{4,3,2,1,0:T(8,128)(2,1)S(1)}, u32[]{:S(2)}) copy-start(bf16[1,32,8,64,128]{4,3,2,1,0:T(8,128)(2,1)S(1)} %local_mix.1.local) | copy-start | bytes 12582916
  42.6 30.8 %copy-start.3 = (bf16[1,32,8,64,128]{4,3,2,1,0:T(8,128)(2,1)S(1)}, bf16[1,32,8,64,128]{4,3,2,1,0:T(8,128)(2,1)}, u32[]{:S(2)}) copy-start(bf16[1,32,8,64,128]{4,3,2,1,0:T(8,128)(2,1)} %copy-done.2) | copy-start | bytes 12582916
  42.6 30.8 %copy-start.9 = (bf16[1,32,8,64,128]{4,3,2,1,0:T(8,128)(2,1)S(1)}, bf16[1,32,8,64,128]{4,3,2,1,0:T(8,128)(2,1)}, u32[]{:S(2)}) copy-start(bf16[1,32,8,64,128]{4,3,2,1,0:T(8,128)(2,1)} %cot.1) | copy-start | bytes 12582916
  42.7 30.8 %copy-start.10 = (bf16[512,256]{1,0:T(8,128)(2,1)S(1)}, bf16[512,256]{1,0:T(8,128)(2,1)}, u32[]{:S(2)}) copy-start(bf16[512,256]{1,0:T(8,128)(2,1)} %constant.17.clone.right_x) | copy-start | bytes 786436
  42.7 30.8 %copy-start.11 = (bf16[128,512]{1,0:T(8,128)(2,1)S(1)}, bf16[128,512]{1,0:T(8,128)(2,1)}, u32[]{:S(2)}) copy-start(bf16[128,512]{1,0:T(8,128)(2,1)} %constant.18.clone.left_y) | copy-start | bytes 393220
  42.7 30.8 %copy-start.12 = (bf16[128,512]{1,0:T(8,128)(2,1)S(1)}, bf16[128,512]{1,0:T(8,128)(2,1)}, u32[]{:S(2)}) copy-start(bf16[128,512]{1,0:T(8,128)(2,1)} %constant.19.clone.half_y) | copy-start | bytes 393220
  42.7 30.8 %copy-start.13 = (bf16[128,256]{1,0:T(8,128)(2,1)S(1)}, bf16[128,256]{1,0:T(8,128)(2,1)}, u32[]{:S(2)}) copy-start(bf16[128,256]{1,0:T(8,128)(2,1)} %constant.16.clone.left_x) | copy-start | bytes 196612
  73.5 33.4 %copy-start.4 = (f32[2,2,32,32,32]{4,3,2,1,0:T(8,128)S(1)}, f32[2,2,32,32,32]{4,3,2,1,0:T(8,128)}, u32[]{:S(2)}) copy-start(f32[2,2,32,32,32]{4,3,2,1,0:T(8,128)} %moment.1) | copy-start | bytes 1572868
  73.5 33.4 %copy-start.5 = (f32[2,2,32,32,32]{4,3,2,1,0:T(8,128)S(1)}, f32[2,2,32,32,32]{4,3,2,1,0:T(8,128)}, u32[]{:S(2)}) copy-start(f32[2,2,32,32,32]{4,3,2,1,0:T(8,128)} %second.1) | copy-start | bytes 1572868

commit v3 on v2

v3 whole, which is shorter than its diff:
```python
import jax
import jax.numpy as jnp
import ml_dtypes
import numpy as np
from jax import lax
from jax.experimental import pallas as pl
from jax.experimental.pallas import tpu as pltpu
from jax.sharding import PartitionSpec as P

beta_one = 0.9
beta_two = 0.999
learn_rate = 0.001
decay_rate = 0.1
adam_eps = 1e-08
adam_step = 1000.0

F32 = jnp.float32
BF16 = jnp.bfloat16
MIB = 1024 * 1024


def table(length, modes=16):
    grid = np.arange(length, dtype=np.float32)[:, None]
    index = np.arange(2 * modes, dtype=np.float32)[None, :]
    freq = np.where(index < modes, index, index - np.float32(modes - 1)).astype(np.float32)
    phase = (np.float32(2.0 * np.pi) * freq * grid / np.float32(length)).astype(np.float32)
    values = np.where(index < modes, np.cos(phase), np.sin(phase)) * np.sqrt(np.float32(2.0 / length))
    return values.astype(np.float32).astype(ml_dtypes.bfloat16).astype(np.float32)


def constants():
    bx, by, bz = table(64), table(128), table(128)
    left_x = np.einsum("xa,cd->acdx", bx, np.eye(4)).reshape(128, 256)
    right_y = np.einsum("yb,qr->qybr", by, np.eye(4)).reshape(512, 128)
    left_z = np.einsum("nqtk,bd->btkndq", bz.reshape(16, 4, 2, 32), np.eye(2)).reshape(128, 128)
    order = np.eye(128).reshape(2, 2, 8, 4, 128).transpose(0, 2, 1, 3, 4).reshape(128, 128).T
    low = lambda v: jnp.asarray(np.ascontiguousarray(v).astype(ml_dtypes.bfloat16))
    tables = (left_x, left_x.T, left_x * 0.5, right_y, right_y.T, left_z, left_z.T, order, order.T)
    return [low(v) for v in tables]


def dot(a, b):
    return lax.dot_general(a, b, (((1,), (0,)), ((), ())), preferred_element_type=F32)


def dot_nt(a, b):
    return lax.dot_general(a, b, (((1,), (1,)), ((), ())), preferred_element_type=F32)


def whole(shape):
    zeros = (0,) * len(shape)
    return pl.BlockSpec(shape, lambda i: zeros)


def resident():
    return pl.BlockSpec(memory_space=pltpu.VMEM)


def outside():
    return pl.BlockSpec(memory_space=pl.ANY)


def call(kernel, grid, in_specs, out_specs, out_shape, scratch, flops, name, vmem):
    return pl.pallas_call(
        kernel,
        grid=(grid,),
        in_specs=in_specs,
        out_specs=out_specs,
        out_shape=out_shape,
        scratch_shapes=scratch,
        compiler_params=pltpu.CompilerParams(vmem_limit_bytes=vmem * MIB),
        cost_estimate=pl.CostEstimate(flops=flops, bytes_accessed=8 << 20, transcendentals=0),
        name=name,
    )


def store_modes(planar, right_y, left_x, start, planes):
    zero = jnp.zeros((512, 128), BF16)
    both = jnp.concatenate(
        [jnp.concatenate([right_y, zero], axis=1), jnp.concatenate([zero, right_y], axis=1)], axis=0
    )
    modes = dot(jnp.concatenate(planes, axis=1), both).astype(BF16)
    for i in range(modes.shape[0] // 256):
        product = dot(left_x, modes[i * 256 : (i + 1) * 256]).reshape(16, 8, 256)
        for z2 in range(2):
            planar[:, z2, start + i] = product[:, :, z2 * 128 : (z2 + 1) * 128]


def store_messages(planar, out):
    for pair in range(8):
        tiles = [planar[ap].reshape(128, 128).T.reshape(16, 8, 128) for ap in (pair * 2, pair * 2 + 1)]
        out[:, pair] = jnp.concatenate(tiles, axis=1).astype(BF16)


def forward_kernel(field, left_x, right_y, out, planar):
    step = pl.program_id(0)
    planes = [field[0, :, zq * 2 + z2].reshape(512, 128) for z2 in range(2) for zq in range(4)]
    store_modes(planar, right_y[...], left_x[...], step * 2, planes)

    @pl.when(step == 3)
    def _():
        store_messages(planar, out)


PLANAR = (16, 2, 8, 8, 128)
MESSAGES = (16, 8, 16, 128)


def forward(field, left_x, right_y):
    return call(
        forward_kernel,
        4,
        [
            pl.BlockSpec((1, 8, 8, 64, 128), lambda i: (0, i, 0, 0, 0)),
            whole((128, 256)),
            whole((512, 128)),
        ],
        whole(MESSAGES),
        jax.ShapeDtypeStruct(MESSAGES, BF16),
        [pltpu.VMEM(PLANAR, F32)],
        1 << 31,
        "planes_to_modes",
        60,
    )(field, left_x, right_y).reshape(2048, 128)


def local_kernel(field, weight, out, left_c):
    @pl.when(pl.program_id(0) == 0)
    def _():
        row = lax.broadcasted_iota(jnp.int32, (256, 32), 0)
        column = lax.broadcasted_iota(jnp.int32, (256, 32), 1)
        spread = jnp.where(row // 8 == column, 1.0, 0.0).astype(BF16)
        rows = dot_nt(spread, weight[...]).astype(BF16)
        row = lax.broadcasted_iota(jnp.int32, (256, 256), 0)
        column = lax.broadcasted_iota(jnp.int32, (256, 256), 1)
        left_c[...] = jnp.where(row % 8 == column % 8, dot_nt(rows, spread), 0.0).astype(BF16)

    for xg in range(4):
        cols = []
        for z2 in range(2):
            rows = field[0, :, z2, xg * 16 : (xg + 1) * 16, :].astype(F32)
            cols.append(rows.reshape(32, 2, 8, 128))
        halves = []
        for half in range(2):
            block = jnp.concatenate([c[:, half].reshape(256, 128) for c in cols], axis=1)
            halves.append(dot(left_c[...], block.astype(BF16)))
        for z2 in range(2):
            parts = [h[:, z2 * 128 : (z2 + 1) * 128].reshape(32, 1, 8, 128) for h in halves]
            both = jnp.concatenate(parts, axis=1).reshape(32, 16, 128)
            out[0, :, z2, xg * 16 : (xg + 1) * 16, :] = both.astype(BF16)


def local_mix(field, weight):
    plane = pl.BlockSpec((1, 32, 2, 64, 128), lambda i: (0, 0, i, 0, 0))
    return call(
        local_kernel,
        4,
        [plane, whole((32, 32))],
        plane,
        jax.ShapeDtypeStruct(field.shape, BF16),
        [pltpu.VMEM((256, 256), BF16)],
        1 << 31,
        "local_mix",
        60,
    )(field, weight)


def spread_kernel(weight, order, order_t, out):
    rows = []
    for b2 in range(2):
        for a2 in range(2):
            r = b2 * 2 + a2
            flat = weight[a2, b2].reshape(256, 32).astype(BF16)
            rows.append(dot(flat, order[r * 32 : (r + 1) * 32, :]).astype(BF16))
    for k in range(8):
        block = jnp.concatenate([v[k * 32 : (k + 1) * 32] for v in rows], axis=0)
        out[k] = dot(order_t[...], block).astype(BF16)


def spread_weights(weight, order, order_t):
    return call(
        spread_kernel,
        4,
        [pl.BlockSpec((2, 2, 8, 32, 32), lambda i: (0, 0, i, 0, 0)), whole((128, 128)), whole((128, 128))],
        pl.BlockSpec((8, 128, 128), lambda i: (i, 0, 0)),
        jax.ShapeDtypeStruct((32, 128, 128), BF16),
        [],
        1 << 28,
        "spread_weights",
        16,
    )(weight, order, order_t)


def z_modes(received, left_z, spectrum):
    low_half = lax.broadcasted_iota(jnp.int32, (32, 128), 1) < 64
    for pair in range(8):
        both = [received[s * 128 : (s + 1) * 128, :] for s in (2 * pair, 2 * pair + 1)]
        product = dot(left_z, jnp.concatenate(both, axis=1))
        for odd in range(2):
            p = product[:, odd * 128 : (odd + 1) * 128]
            stay = jnp.where(low_half, p[0:32], p[96:128])
            move = jnp.where(low_half, p[64:96], p[32:64])
            spectrum[pl.ds(2 * pair + odd, 32, stride=16), :] = stay + pltpu.roll(move, 64, axis=1)


def mix_kernel(received, weights, left_z, right_z, out, kept, spectrum, mixed):
    z_modes(received, left_z[...], spectrum)
    kept[...] = spectrum[...].astype(BF16)
    for k in range(32):
        rows = slice(k * 16, (k + 1) * 16)
        mixed[rows, :] = dot(spectrum[rows, :].astype(BF16), weights[k])
    low_half = lax.broadcasted_iota(jnp.int32, (32, 128), 1) < 64
    for pair in range(8):
        blocks = []
        for s in (2 * pair, 2 * pair + 1):
            y = mixed[pl.ds(s, 32, stride=16), :]
            turned = pltpu.roll(y, 64, axis=1)
            stack = [
                jnp.where(low_half, y, 0.0),
                jnp.where(low_half, 0.0, turned),
                jnp.where(low_half, turned, 0.0),
                jnp.where(low_half, 0.0, y),
            ]
            blocks.append(jnp.concatenate(stack, axis=0).astype(BF16))
        product = dot(right_z[...], jnp.concatenate(blocks, axis=1)).astype(BF16)
        for odd in range(2):
            s = 2 * pair + odd
            out[s * 128 : (s + 1) * 128, :] = product[:, odd * 128 : (odd + 1) * 128]


def mix(received, weights, left_z, right_z):
    return call(
        mix_kernel,
        1,
        [whole((2048, 128)), whole((32, 128, 128)), whole((128, 128)), whole((128, 128))],
        [whole((2048, 128)), whole((512, 128))],
        [jax.ShapeDtypeStruct((2048, 128), BF16), jax.ShapeDtypeStruct((512, 128), BF16)],
        [pltpu.VMEM((512, 128), F32), pltpu.VMEM((512, 128), F32)],
        1 << 34,
        "mix_modes",
        16,
    )(received, weights, left_z, right_z)


def gelu_pull(v, cot):
    k = 0.7978845608028654
    square = v * v
    t = jnp.tanh(v * (square * low(k * 0.044715) + low(k)))
    slope = v * (square * low(3.0 * k * 0.044715) + low(k))
    one = low(1.0)
    return cot * ((one + t) * (one + (one - t) * slope))


def low(value):
    return jnp.asarray(value, BF16)


def middle_kernel(received, local, cot, half_x, right_x, left_y, right_y, out, coefficients, planar):
    for pair in range(8):
        both = received[:, pair].astype(F32).reshape(16, 2, 8, 128)
        tiles = [both[:, odd].reshape(128, 128).T.reshape(2, 8, 8, 128) for odd in range(2)]
        coefficients[:, :, pair] = jnp.concatenate(tiles, axis=2).astype(BF16)

    def some(step, carry):
        spectral = []
        for i in range(2):
            halves = [coefficients[z2, step * 2 + i].reshape(128, 128) for z2 in range(2)]
            spectral.append(dot(right_x[...], jnp.concatenate(halves, axis=1)).astype(BF16))
        spectral = jnp.concatenate(spectral, axis=0)
        channels = pl.ds(step * 8, 8)
        planes = []
        for z2 in range(2):
            pre = dot(spectral[:, z2 * 128 : (z2 + 1) * 128], left_y[...]).astype(BF16)
            for zq in range(4):
                z = zq * 2 + z2
                v = pre[:, zq * 128 : (zq + 1) * 128] + local[0, channels, z].reshape(512, 128)
                planes.append(gelu_pull(v, cot[0, channels, z].reshape(512, 128)))
        store_modes(planar, right_y[...], half_x[...], step * 2, planes)
        return carry

    lax.fori_loop(0, 4, some, 0)
    store_messages(planar, out)


def middle(received, local, cot, half_x, right_x, left_y, right_y):
    return call(
        middle_kernel,
        1,
        [
            whole(MESSAGES),
            resident(),
            resident(),
            whole((128, 256)),
            whole((256, 128)),
            whole((128, 512)),
            whole((512, 128)),
        ],
        whole(MESSAGES),
        jax.ShapeDtypeStruct(MESSAGES, BF16),
        [pltpu.VMEM((2, 8, 8, 16, 128), BF16), pltpu.VMEM(PLANAR, F32)],
        1 << 32,
        "gelu_gradient",
        32,
    )(received.reshape(MESSAGES), local, cot, half_x, right_x, left_y, right_y).reshape(2048, 128)


STEP = 8


def update_kernel(
    received, kept, left_z, order_t, weight, moment, second, new_weight, new_moment, new_second, spectrum, results, sems
):
    z_modes(received, left_z[...], spectrum)

    def copies(step):
        some = pl.ds(step * STEP, STEP)
        return [
            pltpu.make_async_copy(results.at[i, :, :, some], target.at[:, :, some], sems.at[i, step])
            for i, target in enumerate((new_weight, new_moment, new_second))
        ]

    for step in range(32 // STEP):
        rows = slice(step * STEP * 16, (step + 1) * STEP * 16)
        left = dot(kept[rows, :], order_t[...]).T.astype(BF16)
        right = dot(spectrum[rows, :].astype(BF16), order_t[...]).astype(BF16)
        zero = jnp.zeros((16, 128), BF16)
        columns = []
        for i in range(STEP):
            tiles = [zero] * STEP
            tiles[i] = right[i * 16 : (i + 1) * 16]
            columns.append(jnp.concatenate(tiles, axis=0))
        product = dot(left, jnp.concatenate(columns, axis=1))
        for i in range(STEP):
            k = step * STEP + i
            for b2 in range(2):
                for a2 in range(2):
                    r = b2 * 2 + a2
                    block = product[r * 32 : (r + 1) * 32, i * 128 : (i + 1) * 128]
                    if r:
                        block = pltpu.roll(block, 128 - 32 * r, axis=1)
                    grad = block[:, :32]
                    w = weight[a2, b2, k]
                    first = beta_one * moment[a2, b2, k] + (1.0 - beta_one) * grad
                    square = beta_two * second[a2, b2, k] + (1.0 - beta_two) * grad * grad
                    first_hat = first / (1.0 - beta_one**adam_step)
                    second_hat = square / (1.0 - beta_two**adam_step)
                    results[1, a2, b2, k] = first
                    results[2, a2, b2, k] = square
                    results[0, a2, b2, k] = w - learn_rate * (
                        first_hat / (jnp.sqrt(second_hat) + adam_eps) + decay_rate * w
                    )
        for copy in copies(step):
            copy.start()
    for step in range(32 // STEP):
        for copy in copies(step):
            copy.wait()


def update(received, kept, left_z, order_t, weight, moment, second):
    return call(
        update_kernel,
        1,
        [whole((2048, 128)), whole((512, 128)), whole((128, 128)), whole((128, 128))] + [resident()] * 3,
        [outside()] * 3,
        [jax.ShapeDtypeStruct(weight.shape, F32)] * 3,
        [
            pltpu.VMEM((512, 128), F32),
            pltpu.VMEM((3,) + weight.shape, F32),
            pltpu.SemaphoreType.DMA((3, 32 // STEP)),
        ],
        1 << 28,
        "adam_update",
        24,
    )(received, kept, left_z, order_t, weight, moment, second)


def exchange(messages):
    return lax.all_to_all(messages, ("dp", "mp"), split_axis=0, concat_axis=0, tiled=True)


def body(field, cotangent, spectral_weight, first_moment, second_moment, local_weight):
    left_x, right_x, half_x, right_y, left_y, left_z, right_z, order, order_t = constants()
    received = exchange(forward(field, left_x, right_y))
    local = local_mix(field, local_weight)
    spread = spread_weights(spectral_weight, order, order_t)
    received, local, spread = lax.optimization_barrier((received, local, spread))
    mixed, kept = mix(received, spread, left_z, right_z)
    received = exchange(mixed)
    received = exchange(middle(received, local, cotangent, half_x, right_x, left_y, right_y))
    return tuple(update(received, kept, left_z, order_t, spectral_weight, first_moment, second_moment))


def solution(mesh):
    spread = P("dp", None, "mp", None, None)
    modes = P("mp", "dp", None, None, None)
    return jax.shard_map(
        body,
        mesh=mesh,
        in_specs=(spread, spread, modes, modes, modes, P()),
        out_specs=(modes, modes, modes),
        check_vma=False,
    )
```

time: 112 us -> 107 us (0.955)
  local copies, waits for them, and re-layouts: 8.35 us -> 0.08 us
  waiting for transfers between devices: 6.14 us -> 12.4 us
  blocking collectives: 54.3 us -> 51.7 us
  other arithmetic: 1.53 us -> 0 us
  Pallas kernels: 24 us -> 25.2 us
    all_to_all x1, waiting for transfers between devices: 6.14 us -> 12.4 us  [exchange(): lax.all_to_all(messages, ('dp', 'mp'), split_axis=0, concat_axis=0, tiled...]
    unnamed x32 -> x26, local copies, waits for them, and re-layouts: 4.21 us -> 0.08 us
    mul x1 -> x0, local copies, waits for them, and re-layouts: 4.05 us -> none  [body(): local_weight.T[:, None, :, None] * eye[None, :, None, :]]
    pallas_call x3, Pallas kernels: 12.4 us -> 15.7 us  [the longest x1 5.89 us: local_mix(): call(local_kernel, 4, [plane, whole((32, 32))], plane, jax.ShapeDtypeStru...]
    all_to_all x2, blocking collectives: 54.3 us -> 51.7 us  [exchange(): lax.all_to_all(messages, ('dp', 'mp'), split_axis=0, concat_axis=0, tiled...]
    pallas_call x1, Pallas kernels: 7.57 us -> 5.43 us  [middle(): call(middle_kernel, 1, [whole(MESSAGES), resident(), resident(), whole((1...]
    mul x1 -> x0, other arithmetic: 1.53 us -> none  [body(): local_weight.T[:, None, :, None] * eye[None, :, None, :]]
  transfers between devices with their start and end apart: 1 -> 1, of which waited for: 1 -> 1; matrix products, arithmetic and copies ran while one was open for 5% -> 0% of each run, Pallas kernels for 4% -> 7%
where the time goes in v3:
time: 107 us
  blocking collectives  51.7 us (48%)
  Pallas kernels  25.2 us (24%)
  starting transfers between devices  16.7 us (16%)
  waiting for transfers between devices  12.4 us (12%)
    all_to_all x2, blocking collectives, exchange(): lax.all_to_all(messages, ('dp', 'mp'), split_axis=0, concat_axis=0, tiled...  51.7 us
    all_to_all x1, starting transfers between devices, exchange(): lax.all_to_all(messages, ('dp', 'mp'), split_axis=0, concat_axis=0, tiled...  16.7 us
    all_to_all x1, waiting for transfers between devices, exchange(): lax.all_to_all(messages, ('dp', 'mp'), split_axis=0, concat_axis=0, tiled...  12.4 us
    pallas_call x1, Pallas kernels, local_mix(): call(local_kernel, 4, [plane, whole((32, 32))], plane, jax.ShapeDtypeStru...  5.89 us
    pallas_call x1, Pallas kernels, forward(): call(forward_kernel, 4, [pl.BlockSpec((1, 8, 8, 64, 128), lambda i: (0, i...  5.61 us
    pallas_call x1, Pallas kernels, middle(): call(middle_kernel, 1, [whole(MESSAGES), resident(), resident(), whole((1...  5.43 us
    pallas_call x1, Pallas kernels, update(): call(update_kernel, 1, [whole((2048, 128)), whole((512, 128)), whole((128...  4.21 us
    pallas_call x1, Pallas kernels, mix(): call(mix_kernel, 1, [whole((2048, 128)), whole((32, 128, 128)), whole((12...  2.28 us
  transfers between devices with their start and end apart: 1, of which 1 were waited for; matrix products, arithmetic and copies ran while one was open for 0% of the time, Pallas kernels for 7%

profile of v3, /device:TPU:1, one launch (start us, length us, event | category | flops | bytes accessed | tf_op | source)
XLA Modules:
  0.0 106.8 jit_solution(1873391669803355276)
XLA Ops:
  0.6 0.0 copy-start.4
  0.6 0.0 copy-start.6
  0.7 0.0 copy-start
  0.7 5.6 %planes_to_modes.1 = bf16[16,8,16,128]{3,2,1,0:T(8,128)(2,1)} custom-call(bf16[1,32,8,64,128]{4,3,2,1,0:T(8,128)(2,1)} %field.3, bf16[128,256]{1,0:T(8,128)(2,1)} %constant.18.clone.left_x, bf16[512,128]{1,0:T(8,128)(2,1)} %constant.21.clone.right_y), custom_call_target="tpu_custom_call" | custom-call | flops 2147483648 | bytes 8388608 | tf_op jit(solution)/shard_map/planes_to_modes/pallas_call | solution.py:110
  6.3 16.7 %all-to-all-start = ((bf16[256,8,128]{2,1,0:T(8,128)(2,1)}), bf16[256,8,128]{2,1,0:T(8,128)(2,1)}, u32[]{:S(2)}, u32[]{:S(2)}) async-start(bf16[256,8,128]{2,1,0:T(8,128)(2,1)} %bitcast.10), calls=%async_computation | async-start | bytes 1048576 | tf_op jit(solution)/shard_map/all_to_all | solution.py:378
  22.9 0.0 copy-done.4
  23.0 0.0 copy-done.6
  23.0 0.0 copy-done
  23.0 1.8 %spread_weights.1.weights = bf16[32,128,128]{2,1,0:T(8,128)(2,1)S(1)} custom-call(f32[2,2,32,32,32]{4,3,2,1,0:T(8,128)S(1)} %copy-done, bf16[128,128]{1,0:T(8,128)(2,1)S(1)} %copy-done.6, bf16[128,128]{1,0:T(8,128)(2,1)S(1)} %copy-done.4), custom_call_target="tpu_custom_call" | custom-call | flops 268435456 | bytes 8388608 | tf_op jit(solution)/shard_map/spread_weights/pallas_call | solution.py:181
  24.7 0.0 copy-start.5
  24.7 0.0 copy-start.12
  24.8 5.9 %local_mix.1.local = bf16[1,32,8,64,128]{4,3,2,1,0:T(8,128)(2,1)} custom-call(bf16[1,32,8,64,128]{4,3,2,1,0:T(8,128)(2,1)} %field.3, bf16[32,32]{1,0:T(8,128)(2,1)} %weight.3), custom_call_target="tpu_custom_call" | custom-call | flops 2147483648 | bytes 8388608 | tf_op jit(solution)/shard_map/local_mix/pallas_call | solution.py:155
  30.6 12.4 %all-to-all-done = bf16[256,8,128]{2,1,0:T(8,128)(2,1)} async-done(((bf16[256,8,128]{2,1,0:T(8,128)(2,1)}), bf16[256,8,128]{2,1,0:T(8,128)(2,1)}, u32[]{:S(2)}, u32[]{:S(2)}) %all-to-all-start) | async-done | bytes 524320 | tf_op jit(solution)/shard_map/all_to_all | solution.py:378
  43.1 0.0 copy-done.5
  43.1 0.0 copy-done.12
  43.1 0.0 copy-start.1
  43.1 0.0 copy-start.7
  43.1 0.0 copy-start.8
  43.1 0.0 copy-start.9
  43.1 0.0 copy-start.10
  43.1 0.0 copy-start.11
  43.2 2.3 %mix_modes.1 = (bf16[2048,128]{1,0:T(8,128)(2,1)S(1)}, bf16[512,128]{1,0:T(8,128)(2,1)S(1)}) custom-call(bf16[2048,128]{1,0:T(8,128)(2,1)} %bitcast.1.received, bf16[32,128,128]{2,1,0:T(8,128)(2,1)S(1)} %spread_weights.1.weights, bf16[128,128]{1,0:T(8,128)(2,1)S(1)} %copy-done.5, bf16[128,128]{1,0:T(8,128)(2,1)S(1)} %copy-done.12), custom_call_target="tpu_custom_call" | custom-call | flops 17179869184 | bytes 8388608 | tf_op jit(solution)/shard_map/mix_modes/pallas_call | solution.py:232
  45.4 25.8 %all_to_all.32 = bf16[256,8,128]{2,1,0:T(8,128)(2,1)S(1)} all-to-all(bf16[256,8,128]{2,1,0:T(8,128)(2,1)S(1)} %bitcast.9), channel_id=1, replica_groups=mesh['dp'=16,'mp'=16] {'dp','mp'}, dimensions={0} | all-to-all | bytes 1048576 | tf_op jit(solution)/shard_map/all_to_all | solution.py:378
  71.3 0.0 copy-done.1
  71.3 0.0 copy-done.7
  71.3 0.0 copy-done.8
  71.3 0.0 copy-done.9
  71.3 0.0 copy-done.10
  71.3 0.0 copy-done.11
  71.3 0.0 copy-start.2
  71.3 0.0 copy-start.3
  71.3 5.4 %gelu_gradient.1 = bf16[16,8,16,128]{3,2,1,0:T(8,128)(2,1)S(1)} custom-call(bf16[16,8,16,128]{3,2,1,0:T(8,128)(2,1)S(1)} %bitcast.7, bf16[1,32,8,64,128]{4,3,2,1,0:T(8,128)(2,1)S(1)} %copy-done.1, bf16[1,32,8,64,128]{4,3,2,1,0:T(8,128)(2,1)S(1)} %copy-done.7, bf16[128,256]{1,0:T(8,128)(2,1)S(1)} %copy-done.10, bf16[256,128]{1,0:T(8,128)(2,1)S(1)} %copy-done.11, ...), custom_call_target="tpu_custom_call" | custom-call | flops 4294967296 | bytes 8388608 | tf_op jit(solution)/shard_map/gelu_gradient/pallas_call | solution.py:286
  76.8 25.8 %all_to_all.33 = bf16[256,8,128]{2,1,0:T(8,128)(2,1)S(1)} all-to-all(bf16[256,8,128]{2,1,0:T(8,128)(2,1)S(1)} %bitcast.8), channel_id=1, replica_groups=mesh['dp'=16,'mp'=16] {'dp','mp'}, dimensions={0} | all-to-all | bytes 1048576 | tf_op jit(solution)/shard_map/all_to_all | solution.py:378
  102.6 0.0 copy-done.2
  102.6 0.0 copy-done.3
  102.6 4.2 %adam_update.1 = (f32[2,2,32,32,32]{4,3,2,1,0:T(8,128)}, f32[2,2,32,32,32]{4,3,2,1,0:T(8,128)}, f32[2,2,32,32,32]{4,3,2,1,0:T(8,128)}) custom-call(bf16[2048,128]{1,0:T(8,128)(2,1)S(1)} %bitcast.6, bf16[512,128]{1,0:T(8,128)(2,1)S(1)} %get-tuple-element.12.kept, bf16[128,128]{1,0:T(8,128)(2,1)S(1)} %copy-done.5, bf16[128,128]{1,0:T(8,128)(2,1)S(1)} %copy-done.4, ...), custom_call_target="tpu_custom_call" | custom-call | flops 268435456 | bytes 8388608 | tf_op jit(solution)/shard_map/adam_update/pallas_call | solution.py:360
Async XLA Ops:
  0.6 22.3 %copy-start.4 = (bf16[128,128]{1,0:T(8,128)(2,1)S(1)}, bf16[128,128]{1,0:T(8,128)(2,1)}, u32[]{:S(2)}) copy-start(bf16[128,128]{1,0:T(8,128)(2,1)} %constant.26.clone.order_t) | copy-start | bytes 98308
  0.6 22.3 %copy-start.6 = (bf16[128,128]{1,0:T(8,128)(2,1)S(1)}, bf16[128,128]{1,0:T(8,128)(2,1)}, u32[]{:S(2)}) copy-start(bf16[128,128]{1,0:T(8,128)(2,1)} %constant.25.clone.order) | copy-start | bytes 98308
  0.7 22.3 %copy-start = (f32[2,2,32,32,32]{4,3,2,1,0:T(8,128)S(1)}, f32[2,2,32,32,32]{4,3,2,1,0:T(8,128)}, u32[]{:S(2)}) copy-start(f32[2,2,32,32,32]{4,3,2,1,0:T(8,128)} %weight.5) | copy-start | bytes 1572868
  6.3 36.8 %all-to-all-start = ((bf16[256,8,128]{2,1,0:T(8,128)(2,1)}), bf16[256,8,128]{2,1,0:T(8,128)(2,1)}, u32[]{:S(2)}, u32[]{:S(2)}) async-start(bf16[256,8,128]{2,1,0:T(8,128)(2,1)} %bitcast.10), calls=%async_computation | async-start | bytes 1048576 | tf_op jit(solution)/shard_map/all_to_all | solution.py:378
  24.7 18.4 %copy-start.5 = (bf16[128,128]{1,0:T(8,128)(2,1)S(1)}, bf16[128,128]{1,0:T(8,128)(2,1)}, u32[]{:S(2)}) copy-start(bf16[128,128]{1,0:T(8,128)(2,1)} %constant.23.clone.left_z) | copy-start | bytes 98308
  24.7 18.3 %copy-start.12 = (bf16[128,128]{1,0:T(8,128)(2,1)S(1)}, bf16[128,128]{1,0:T(8,128)(2,1)}, u32[]{:S(2)}) copy-start(bf16[128,128]{1,0:T(8,128)(2,1)} %constant.24.clone.right_z) | copy-start | bytes 98308
  43.1 28.2 %copy-start.1 = (bf16[1,32,8,64,128]{4,3,2,1,0:T(8,128)(2,1)S(1)}, bf16[1,32,8,64,128]{4,3,2,1,0:T(8,128)(2,1)}, u32[]{:S(2)}) copy-start(bf16[1,32,8,64,128]{4,3,2,1,0:T(8,128)(2,1)} %local_mix.1.local) | copy-start | bytes 12582916
  43.1 28.2 %copy-start.7 = (bf16[1,32,8,64,128]{4,3,2,1,0:T(8,128)(2,1)S(1)}, bf16[1,32,8,64,128]{4,3,2,1,0:T(8,128)(2,1)}, u32[]{:S(2)}) copy-start(bf16[1,32,8,64,128]{4,3,2,1,0:T(8,128)(2,1)} %cot.1) | copy-start | bytes 12582916
  43.1 28.2 %copy-start.8 = (bf16[512,128]{1,0:T(8,128)(2,1)S(1)}, bf16[512,128]{1,0:T(8,128)(2,1)}, u32[]{:S(2)}) copy-start(bf16[512,128]{1,0:T(8,128)(2,1)} %constant.21.clone.right_y) | copy-start | bytes 393220
  43.1 28.2 %copy-start.9 = (bf16[128,512]{1,0:T(8,128)(2,1)S(1)}, bf16[128,512]{1,0:T(8,128)(2,1)}, u32[]{:S(2)}) copy-start(bf16[128,512]{1,0:T(8,128)(2,1)} %constant.22.clone.left_y) | copy-start | bytes 393220
  43.1 28.2 %copy-start.10 = (bf16[128,256]{1,0:T(8,128)(2,1)S(1)}, bf16[128,256]{1,0:T(8,128)(2,1)}, u32[]{:S(2)}) copy-start(bf16[128,256]{1,0:T(8,128)(2,1)} %constant.20.clone.half_x) | copy-start | bytes 196612
  43.1 28.2 %copy-start.11 = (bf16[256,128]{1,0:T(8,128)(2,1)S(1)}, bf16[256,128]{1,0:T(8,128)(2,1)}, u32[]{:S(2)}) copy-start(bf16[256,128]{1,0:T(8,128)(2,1)} %constant.19.clone.right_x) | copy-start | bytes 196612
  71.3 31.3 %copy-start.2 = (f32[2,2,32,32,32]{4,3,2,1,0:T(8,128)S(1)}, f32[2,2,32,32,32]{4,3,2,1,0:T(8,128)}, u32[]{:S(2)}) copy-start(f32[2,2,32,32,32]{4,3,2,1,0:T(8,128)} %moment.1) | copy-start | bytes 1572868
  71.3 31.3 %copy-start.3 = (f32[2,2,32,32,32]{4,3,2,1,0:T(8,128)S(1)}, f32[2,2,32,32,32]{4,3,2,1,0:T(8,128)}, u32[]{:S(2)}) copy-start(f32[2,2,32,32,32]{4,3,2,1,0:T(8,128)} %second.1) | copy-start | bytes 1572868

commit v4 on v3

--- a/solution.py
+++ b/solution.py
@@ -74,14 +74,17 @@
     )
 
 
-def store_modes(planar, right_y, left_x, start, planes):
+def y_modes(right_y, planes):
     zero = jnp.zeros((512, 128), BF16)
     both = jnp.concatenate(
         [jnp.concatenate([right_y, zero], axis=1), jnp.concatenate([zero, right_y], axis=1)], axis=0
     )
-    modes = dot(jnp.concatenate(planes, axis=1), both).astype(BF16)
-    for i in range(modes.shape[0] // 256):
-        product = dot(left_x, modes[i * 256 : (i + 1) * 256]).reshape(16, 8, 256)
+    return dot(jnp.concatenate(planes, axis=1), both).astype(BF16)
+
+
+def store_modes(planar, modes, left_x, start):
+    for i in range(2):
+        product = dot(left_x, modes[i * 256 : (i + 1) * 256, :]).reshape(16, 8, 256)
         for z2 in range(2):
             planar[:, z2, start + i] = product[:, :, z2 * 128 : (z2 + 1) * 128]
 
@@ -92,36 +95,47 @@
         out[:, pair] = jnp.concatenate(tiles, axis=1).astype(BF16)
 
 
-def forward_kernel(field, left_x, right_y, out, planar):
-    step = pl.program_id(0)
-    planes = [field[0, :, zq * 2 + z2].reshape(512, 128) for z2 in range(2) for zq in range(4)]
-    store_modes(planar, right_y[...], left_x[...], step * 2, planes)
-
-    @pl.when(step == 3)
+def forward_kernel(field, left_x, left_y, out, first):
+    zq = pl.program_id(0)
+    for group in range(4):
+        halves = []
+        for half in range(2):
+            rows = slice(group * 8 + half * 4, group * 8 + half * 4 + 4)
+            block = jnp.concatenate([field[0, rows, z2].reshape(256, 128) for z2 in range(2)], axis=1)
+            halves.append(dot(left_x[...], block).reshape(16, 1, 8, 256))
+        both = jnp.concatenate(halves, axis=1).reshape(16, 16, 256).astype(BF16)
+        for z2 in range(2):
+            first[:, zq, z2, group] = both[:, :, z2 * 128 : (z2 + 1) * 128]
+
+    @pl.when(zq == 3)
     def _():
-        store_messages(planar, out)
+        for pair in range(8):
+            planes = [first[pair * 2 : pair * 2 + 2, q].reshape(256, 128) for q in range(4)]
+            planar = dot_nt(left_y[...], jnp.concatenate(planes, axis=1))
+            tiles = [planar[:, :128].reshape(16, 8, 128), planar[:, 128:].reshape(16, 8, 128)]
+            out[:, pair] = jnp.concatenate(tiles, axis=1).astype(BF16)
 
 
 PLANAR = (16, 2, 8, 8, 128)
 MESSAGES = (16, 8, 16, 128)
 
 
-def forward(field, left_x, right_y):
+def forward(field, left_x, left_y):
     return call(
         forward_kernel,
         4,
         [
-            pl.BlockSpec((1, 8, 8, 64, 128), lambda i: (0, i, 0, 0, 0)),
+            pl.BlockSpec((1, 32, 2, 64, 128), lambda i: (0, 0, i, 0, 0)),
             whole((128, 256)),
-            whole((512, 128)),
+            whole((128, 512)),
         ],
         whole(MESSAGES),
         jax.ShapeDtypeStruct(MESSAGES, BF16),
-        [pltpu.VMEM(PLANAR, F32)],
+        [pltpu.VMEM((16, 4, 2, 4, 16, 128), BF16)],
         1 << 31,
         "planes_to_modes",
         60,
-    )(field, left_x, right_y).reshape(2048, 128)
+    )(field, left_x, left_y).reshape(2048, 128)
 
 
 def local_kernel(field, weight, out, left_c):
@@ -248,25 +262,29 @@
     t = jnp.tanh(v * (square * low(k * 0.044715) + low(k)))
     slope = v * (square * low(3.0 * k * 0.044715) + low(k))
     one = low(1.0)
-    return cot * ((one + t) * (one + (one - t) * slope))
+    return (one + t) * (one + (one - t) * slope) * cot
 
 
 def low(value):
     return jnp.asarray(value, BF16)
 
 
-def middle_kernel(received, local, cot, half_x, right_x, left_y, right_y, out, coefficients, planar):
+def middle_kernel(
+    received, local, cot, half_x, right_x, left_y, right_y, out, coefficients, planar, spectral, modes
+):
     for pair in range(8):
         both = received[:, pair].astype(F32).reshape(16, 2, 8, 128)
         tiles = [both[:, odd].reshape(128, 128).T.reshape(2, 8, 8, 128) for odd in range(2)]
         coefficients[:, :, pair] = jnp.concatenate(tiles, axis=2).astype(BF16)
 
-    def some(step, carry):
-        spectral = []
+    def inverse_x(step):
         for i in range(2):
             halves = [coefficients[z2, step * 2 + i].reshape(128, 128) for z2 in range(2)]
-            spectral.append(dot(right_x[...], jnp.concatenate(halves, axis=1)).astype(BF16))
-        spectral = jnp.concatenate(spectral, axis=0)
+            rows = slice(i * 256, (i + 1) * 256)
+            spectral[rows, :] = dot(right_x[...], jnp.concatenate(halves, axis=1)).astype(BF16)
+
+    def some(step, carry):
+        store_modes(planar, modes, half_x[...], jnp.maximum(step - 1, 0) * 2)
         channels = pl.ds(step * 8, 8)
         planes = []
         for z2 in range(2):
@@ -275,10 +293,14 @@
                 z = zq * 2 + z2
                 v = pre[:, zq * 128 : (zq + 1) * 128] + local[0, channels, z].reshape(512, 128)
                 planes.append(gelu_pull(v, cot[0, channels, z].reshape(512, 128)))
-        store_modes(planar, right_y[...], half_x[...], step * 2, planes)
+        inverse_x(jnp.minimum(step + 1, 3))
+        modes[...] = y_modes(right_y[...], planes)
         return carry
 
+    inverse_x(0)
+    modes[...] = jnp.zeros((512, 256), BF16)
     lax.fori_loop(0, 4, some, 0)
+    store_modes(planar, modes, half_x[...], 6)
     store_messages(planar, out)
 
 
@@ -297,7 +319,12 @@
         ],
         whole(MESSAGES),
         jax.ShapeDtypeStruct(MESSAGES, BF16),
-        [pltpu.VMEM((2, 8, 8, 16, 128), BF16), pltpu.VMEM(PLANAR, F32)],
+        [
+            pltpu.VMEM((2, 8, 8, 16, 128), BF16),
+            pltpu.VMEM(PLANAR, F32),
+            pltpu.VMEM((512, 256), BF16),
+            pltpu.VMEM((512, 256), BF16),
+        ],
         1 << 32,
         "gelu_gradient",
         32,
@@ -380,7 +407,7 @@
 
 def body(field, cotangent, spectral_weight, first_moment, second_moment, local_weight):
     left_x, right_x, half_x, right_y, left_y, left_z, right_z, order, order_t = constants()
-    received = exchange(forward(field, left_x, right_y))
+    received = exchange(forward(field, left_x, left_y))
     local = local_mix(field, local_weight)
     spread = spread_weights(spectral_weight, order, order_t)
     received, local, spread = lax.optimization_barrier((received, local, spread))

time: 107 us -> 106 us (level)
  Pallas kernels: 25.2 us -> 23.8 us
    pallas_call x1, Pallas kernels: 5.43 us -> 4.32 us  [middle(): call(middle_kernel, 1, [whole(MESSAGES), resident(), resident(), whole((1...]
where the time goes in v4:
time: 106 us; the launch traced here: 105 us
  blocking collectives  51.7 us (49%)
  Pallas kernels  23.8 us (22%)
  starting transfers between devices  16.7 us (16%)
  waiting for transfers between devices  12.4 us (12%)
    all_to_all x2, blocking collectives, exchange(): lax.all_to_all(messages, ('dp', 'mp'), split_axis=0, concat_axis=0, tiled...  51.7 us
    all_to_all x1, starting transfers between devices, exchange(): lax.all_to_all(messages, ('dp', 'mp'), split_axis=0, concat_axis=0, tiled...  16.7 us
    all_to_all x1, waiting for transfers between devices, exchange(): lax.all_to_all(messages, ('dp', 'mp'), split_axis=0, concat_axis=0, tiled...  12.4 us
    pallas_call x1, Pallas kernels, local_mix(): call(local_kernel, 4, [plane, whole((32, 32))], plane, jax.ShapeDtypeStru...  5.89 us
    pallas_call x1, Pallas kernels, forward(): call(forward_kernel, 4, [pl.BlockSpec((1, 32, 2, 64, 128), lambda i: (0,...  5.32 us
    pallas_call x1, Pallas kernels, middle(): call(middle_kernel, 1, [whole(MESSAGES), resident(), resident(), whole((1...  4.32 us
    pallas_call x1, Pallas kernels, update(): call(update_kernel, 1, [whole((2048, 128)), whole((512, 128)), whole((128...  4.21 us
    pallas_call x1, Pallas kernels, mix(): call(mix_kernel, 1, [whole((2048, 128)), whole((32, 128, 128)), whole((12...  2.28 us
  transfers between devices with their start and end apart: 1, of which 1 were waited for; matrix products, arithmetic and copies ran while one was open for 0% of the time, Pallas kernels for 7%

profile of v4, /device:TPU:1, one launch (start us, length us, event | category | flops | bytes accessed | tf_op | source)
XLA Modules:
  0.0 105.4 jit_solution(8152097114538219613)
XLA Ops:
  0.6 0.0 copy-start.4
  0.6 0.0 copy-start.6
  0.7 0.0 copy-start
  0.7 5.3 %planes_to_modes.1 = bf16[16,8,16,128]{3,2,1,0:T(8,128)(2,1)} custom-call(bf16[1,32,8,64,128]{4,3,2,1,0:T(8,128)(2,1)} %field.3, bf16[128,256]{1,0:T(8,128)(2,1)} %constant.18.clone.left_x, bf16[128,512]{1,0:T(8,128)(2,1)} %constant.22.clone.left_y), custom_call_target="tpu_custom_call" | custom-call | flops 2147483648 | bytes 8388608 | tf_op jit(solution)/shard_map/planes_to_modes/pallas_call | solution.py:124
  6.0 16.7 %all-to-all-start = ((bf16[256,8,128]{2,1,0:T(8,128)(2,1)}), bf16[256,8,128]{2,1,0:T(8,128)(2,1)}, u32[]{:S(2)}, u32[]{:S(2)}) async-start(bf16[256,8,128]{2,1,0:T(8,128)(2,1)} %bitcast.10), calls=%async_computation | async-start | bytes 1048576 | tf_op jit(solution)/shard_map/all_to_all | solution.py:405
  22.7 0.0 copy-done.4
  22.7 0.0 copy-done.6
  22.7 0.0 copy-done
  22.7 1.7 %spread_weights.1.weights = bf16[32,128,128]{2,1,0:T(8,128)(2,1)S(1)} custom-call(f32[2,2,32,32,32]{4,3,2,1,0:T(8,128)S(1)} %copy-done, bf16[128,128]{1,0:T(8,128)(2,1)S(1)} %copy-done.6, bf16[128,128]{1,0:T(8,128)(2,1)S(1)} %copy-done.4), custom_call_target="tpu_custom_call" | custom-call | flops 268435456 | bytes 8388608 | tf_op jit(solution)/shard_map/spread_weights/pallas_call | solution.py:195
  24.4 0.0 copy-start.5
  24.5 0.0 copy-start.12
  24.5 5.9 %local_mix.1.local = bf16[1,32,8,64,128]{4,3,2,1,0:T(8,128)(2,1)} custom-call(bf16[1,32,8,64,128]{4,3,2,1,0:T(8,128)(2,1)} %field.3, bf16[32,32]{1,0:T(8,128)(2,1)} %weight.3), custom_call_target="tpu_custom_call" | custom-call | flops 2147483648 | bytes 8388608 | tf_op jit(solution)/shard_map/local_mix/pallas_call | solution.py:169
  30.4 12.4 %all-to-all-done = bf16[256,8,128]{2,1,0:T(8,128)(2,1)} async-done(((bf16[256,8,128]{2,1,0:T(8,128)(2,1)}), bf16[256,8,128]{2,1,0:T(8,128)(2,1)}, u32[]{:S(2)}, u32[]{:S(2)}) %all-to-all-start) | async-done | bytes 524320 | tf_op jit(solution)/shard_map/all_to_all | solution.py:405
  42.8 0.0 copy-done.5
  42.8 0.0 copy-done.12
  42.8 0.0 copy-start.1
  42.8 0.0 copy-start.7
  42.8 0.0 copy-start.8
  42.8 0.0 copy-start.9
  42.8 0.0 copy-start.10
  42.9 0.0 copy-start.11
  42.9 2.3 %mix_modes.1 = (bf16[2048,128]{1,0:T(8,128)(2,1)S(1)}, bf16[512,128]{1,0:T(8,128)(2,1)S(1)}) custom-call(bf16[2048,128]{1,0:T(8,128)(2,1)} %bitcast.1.received, bf16[32,128,128]{2,1,0:T(8,128)(2,1)S(1)} %spread_weights.1.weights, bf16[128,128]{1,0:T(8,128)(2,1)S(1)} %copy-done.5, bf16[128,128]{1,0:T(8,128)(2,1)S(1)} %copy-done.12), custom_call_target="tpu_custom_call" | custom-call | flops 17179869184 | bytes 8388608 | tf_op jit(solution)/shard_map/mix_modes/pallas_call | solution.py:246
  45.2 25.8 %all_to_all.32 = bf16[256,8,128]{2,1,0:T(8,128)(2,1)S(1)} all-to-all(bf16[256,8,128]{2,1,0:T(8,128)(2,1)S(1)} %bitcast.9), channel_id=1, replica_groups=mesh['dp'=16,'mp'=16] {'dp','mp'}, dimensions={0} | all-to-all | bytes 1048576 | tf_op jit(solution)/shard_map/all_to_all | solution.py:405
  71.0 0.0 copy-done.1
  71.0 0.0 copy-done.7
  71.0 0.0 copy-done.8
  71.0 0.0 copy-done.9
  71.0 0.0 copy-done.10
  71.0 0.0 copy-done.11
  71.0 0.0 copy-start.2
  71.0 0.0 copy-start.3
  71.1 4.3 %gelu_gradient.1 = bf16[16,8,16,128]{3,2,1,0:T(8,128)(2,1)S(1)} custom-call(bf16[16,8,16,128]{3,2,1,0:T(8,128)(2,1)S(1)} %bitcast.7, bf16[1,32,8,64,128]{4,3,2,1,0:T(8,128)(2,1)S(1)} %copy-done.1, bf16[1,32,8,64,128]{4,3,2,1,0:T(8,128)(2,1)S(1)} %copy-done.7, bf16[128,256]{1,0:T(8,128)(2,1)S(1)} %copy-done.10, bf16[256,128]{1,0:T(8,128)(2,1)S(1)} %copy-done.11, ...), custom_call_target="tpu_custom_call" | custom-call | flops 4294967296 | bytes 8388608 | tf_op jit(solution)/shard_map/gelu_gradient/pallas_call | solution.py:308
  75.4 25.8 %all_to_all.33 = bf16[256,8,128]{2,1,0:T(8,128)(2,1)S(1)} all-to-all(bf16[256,8,128]{2,1,0:T(8,128)(2,1)S(1)} %bitcast.8), channel_id=1, replica_groups=mesh['dp'=16,'mp'=16] {'dp','mp'}, dimensions={0} | all-to-all | bytes 1048576 | tf_op jit(solution)/shard_map/all_to_all | solution.py:405
  101.2 0.0 copy-done.2
  101.2 0.0 copy-done.3
  101.2 4.2 %adam_update.1 = (f32[2,2,32,32,32]{4,3,2,1,0:T(8,128)}, f32[2,2,32,32,32]{4,3,2,1,0:T(8,128)}, f32[2,2,32,32,32]{4,3,2,1,0:T(8,128)}) custom-call(bf16[2048,128]{1,0:T(8,128)(2,1)S(1)} %bitcast.6, bf16[512,128]{1,0:T(8,128)(2,1)S(1)} %get-tuple-element.12.kept, bf16[128,128]{1,0:T(8,128)(2,1)S(1)} %copy-done.5, bf16[128,128]{1,0:T(8,128)(2,1)S(1)} %copy-done.4, ...), custom_call_target="tpu_custom_call" | custom-call | flops 268435456 | bytes 8388608 | tf_op jit(solution)/shard_map/adam_update/pallas_call | solution.py:387
Async XLA Ops:
  0.6 22.0 %copy-start.4 = (bf16[128,128]{1,0:T(8,128)(2,1)S(1)}, bf16[128,128]{1,0:T(8,128)(2,1)}, u32[]{:S(2)}) copy-start(bf16[128,128]{1,0:T(8,128)(2,1)} %constant.26.clone.order_t) | copy-start | bytes 98308
  0.6 22.0 %copy-start.6 = (bf16[128,128]{1,0:T(8,128)(2,1)S(1)}, bf16[128,128]{1,0:T(8,128)(2,1)}, u32[]{:S(2)}) copy-start(bf16[128,128]{1,0:T(8,128)(2,1)} %constant.25.clone.order) | copy-start | bytes 98308
  0.7 22.0 %copy-start = (f32[2,2,32,32,32]{4,3,2,1,0:T(8,128)S(1)}, f32[2,2,32,32,32]{4,3,2,1,0:T(8,128)}, u32[]{:S(2)}) copy-start(f32[2,2,32,32,32]{4,3,2,1,0:T(8,128)} %weight.5) | copy-start | bytes 1572868
  6.0 36.8 %all-to-all-start = ((bf16[256,8,128]{2,1,0:T(8,128)(2,1)}), bf16[256,8,128]{2,1,0:T(8,128)(2,1)}, u32[]{:S(2)}, u32[]{:S(2)}) async-start(bf16[256,8,128]{2,1,0:T(8,128)(2,1)} %bitcast.10), calls=%async_computation | async-start | bytes 1048576 | tf_op jit(solution)/shard_map/all_to_all | solution.py:405
  24.4 18.4 %copy-start.5 = (bf16[128,128]{1,0:T(8,128)(2,1)S(1)}, bf16[128,128]{1,0:T(8,128)(2,1)}, u32[]{:S(2)}) copy-start(bf16[128,128]{1,0:T(8,128)(2,1)} %constant.23.clone.left_z) | copy-start | bytes 98308
  24.5 18.3 %copy-start.12 = (bf16[128,128]{1,0:T(8,128)(2,1)S(1)}, bf16[128,128]{1,0:T(8,128)(2,1)}, u32[]{:S(2)}) copy-start(bf16[128,128]{1,0:T(8,128)(2,1)} %constant.24.clone.right_z) | copy-start | bytes 98308
  42.8 28.2 %copy-start.1 = (bf16[1,32,8,64,128]{4,3,2,1,0:T(8,128)(2,1)S(1)}, bf16[1,32,8,64,128]{4,3,2,1,0:T(8,128)(2,1)}, u32[]{:S(2)}) copy-start(bf16[1,32,8,64,128]{4,3,2,1,0:T(8,128)(2,1)} %local_mix.1.local) | copy-start | bytes 12582916
  42.8 28.2 %copy-start.7 = (bf16[1,32,8,64,128]{4,3,2,1,0:T(8,128)(2,1)S(1)}, bf16[1,32,8,64,128]{4,3,2,1,0:T(8,128)(2,1)}, u32[]{:S(2)}) copy-start(bf16[1,32,8,64,128]{4,3,2,1,0:T(8,128)(2,1)} %cot.1) | copy-start | bytes 12582916
  42.8 28.2 %copy-start.8 = (bf16[128,512]{1,0:T(8,128)(2,1)S(1)}, bf16[128,512]{1,0:T(8,128)(2,1)}, u32[]{:S(2)}) copy-start(bf16[128,512]{1,0:T(8,128)(2,1)} %constant.22.clone.left_y) | copy-start | bytes 393220
  42.8 28.2 %copy-start.9 = (bf16[512,128]{1,0:T(8,128)(2,1)S(1)}, bf16[512,128]{1,0:T(8,128)(2,1)}, u32[]{:S(2)}) copy-start(bf16[512,128]{1,0:T(8,128)(2,1)} %constant.21.clone.right_y) | copy-start | bytes 393220
  42.8 28.2 %copy-start.10 = (bf16[128,256]{1,0:T(8,128)(2,1)S(1)}, bf16[128,256]{1,0:T(8,128)(2,1)}, u32[]{:S(2)}) copy-start(bf16[128,256]{1,0:T(8,128)(2,1)} %constant.20.clone.half_x) | copy-start | bytes 196612
  42.9 28.2 %copy-start.11 = (bf16[256,128]{1,0:T(8,128)(2,1)S(1)}, bf16[256,128]{1,0:T(8,128)(2,1)}, u32[]{:S(2)}) copy-start(bf16[256,128]{1,0:T(8,128)(2,1)} %constant.19.clone.right_x) | copy-start | bytes 196612
  71.0 30.2 %copy-start.2 = (f32[2,2,32,32,32]{4,3,2,1,0:T(8,128)S(1)}, f32[2,2,32,32,32]{4,3,2,1,0:T(8,128)}, u32[]{:S(2)}) copy-start(f32[2,2,32,32,32]{4,3,2,1,0:T(8,128)} %moment.1) | copy-start | bytes 1572868
  71.0 30.2 %copy-start.3 = (f32[2,2,32,32,32]{4,3,2,1,0:T(8,128)S(1)}, f32[2,2,32,32,32]{4,3,2,1,0:T(8,128)}, u32[]{:S(2)}) copy-start(f32[2,2,32,32,32]{4,3,2,1,0:T(8,128)} %second.1) | copy-start | bytes 1572868

commit v5 on v4

--- a/solution.py
+++ b/solution.py
@@ -95,47 +95,61 @@
         out[:, pair] = jnp.concatenate(tiles, axis=1).astype(BF16)
 
 
-def forward_kernel(field, left_x, left_y, out, first):
-    zq = pl.program_id(0)
-    for group in range(4):
-        halves = []
-        for half in range(2):
-            rows = slice(group * 8 + half * 4, group * 8 + half * 4 + 4)
-            block = jnp.concatenate([field[0, rows, z2].reshape(256, 128) for z2 in range(2)], axis=1)
-            halves.append(dot(left_x[...], block).reshape(16, 1, 8, 256))
-        both = jnp.concatenate(halves, axis=1).reshape(16, 16, 256).astype(BF16)
-        for z2 in range(2):
-            first[:, zq, z2, group] = both[:, :, z2 * 128 : (z2 + 1) * 128]
-
-    @pl.when(zq == 3)
-    def _():
-        for pair in range(8):
-            planes = [first[pair * 2 : pair * 2 + 2, q].reshape(256, 128) for q in range(4)]
-            planar = dot_nt(left_y[...], jnp.concatenate(planes, axis=1))
-            tiles = [planar[:, :128].reshape(16, 8, 128), planar[:, 128:].reshape(16, 8, 128)]
-            out[:, pair] = jnp.concatenate(tiles, axis=1).astype(BF16)
+def forward_kernel(field, left_x, right_y, out, buffer, left_buffer, right_buffer, planar, sems, table_sems):
+    def copy(part):
+        rows = pl.ds(part * 8, 8)
+        return pltpu.make_async_copy(field.at[0, rows], buffer.at[rows], sems.at[part])
+
+    tables = [
+        pltpu.make_async_copy(right_y, right_buffer, table_sems.at[0]),
+        pltpu.make_async_copy(left_x, left_buffer, table_sems.at[1]),
+    ]
+    copy(0).start()
+    for table_copy in tables:
+        table_copy.start()
+    copy(1).start()
+    for table_copy in tables:
+        table_copy.wait()
+
+    def some(step, carry):
+        copy(step).wait()
+
+        @pl.when(step < 2)
+        def _():
+            copy(step + 2).start()
+
+        block = buffer[pl.ds(step * 8, 8)]
+        planes = [block[:, zq * 2 + z2].reshape(512, 128) for z2 in range(2) for zq in range(4)]
+        store_modes(planar, y_modes(right_buffer[...], planes), left_buffer[...], step * 2)
+        return carry
+
+    lax.fori_loop(0, 4, some, 0)
+    store_messages(planar, out)
 
 
 PLANAR = (16, 2, 8, 8, 128)
 MESSAGES = (16, 8, 16, 128)
 
 
-def forward(field, left_x, left_y):
+def forward(field, left_x, right_y):
     return call(
         forward_kernel,
-        4,
-        [
-            pl.BlockSpec((1, 32, 2, 64, 128), lambda i: (0, 0, i, 0, 0)),
-            whole((128, 256)),
-            whole((128, 512)),
-        ],
+        1,
+        [outside()] * 3,
         whole(MESSAGES),
         jax.ShapeDtypeStruct(MESSAGES, BF16),
-        [pltpu.VMEM((16, 4, 2, 4, 16, 128), BF16)],
+        [
+            pltpu.VMEM((32, 8, 64, 128), BF16),
+            pltpu.VMEM((128, 256), BF16),
+            pltpu.VMEM((512, 128), BF16),
+            pltpu.VMEM(PLANAR, F32),
+            pltpu.SemaphoreType.DMA((4,)),
+            pltpu.SemaphoreType.DMA((2,)),
+        ],
         1 << 31,
         "planes_to_modes",
         60,
-    )(field, left_x, left_y).reshape(2048, 128)
+    )(field, left_x, right_y).reshape(2048, 128)
 
 
 def local_kernel(field, weight, out, left_c):
@@ -331,7 +345,7 @@
     )(received.reshape(MESSAGES), local, cot, half_x, right_x, left_y, right_y).reshape(2048, 128)
 
 
-STEP = 8
+STEP = 16
 
 
 def update_kernel(
@@ -366,16 +380,15 @@
                     if r:
                         block = pltpu.roll(block, 128 - 32 * r, axis=1)
                     grad = block[:, :32]
-                    w = weight[a2, b2, k]
                     first = beta_one * moment[a2, b2, k] + (1.0 - beta_one) * grad
                     square = beta_two * second[a2, b2, k] + (1.0 - beta_two) * grad * grad
-                    first_hat = first / (1.0 - beta_one**adam_step)
-                    second_hat = square / (1.0 - beta_two**adam_step)
                     results[1, a2, b2, k] = first
                     results[2, a2, b2, k] = square
-                    results[0, a2, b2, k] = w - learn_rate * (
-                        first_hat / (jnp.sqrt(second_hat) + adam_eps) + decay_rate * w
-                    )
+                    second_hat = square * (1.0 / (1.0 - beta_two**adam_step))
+                    root = second_hat * lax.rsqrt(second_hat)
+                    scaled = first * (learn_rate / (1.0 - beta_one**adam_step))
+                    kept_weight = weight[a2, b2, k] * (1.0 - learn_rate * decay_rate)
+                    results[0, a2, b2, k] = kept_weight - scaled / (root + adam_eps)
         for copy in copies(step):
             copy.start()
     for step in range(32 // STEP):
@@ -407,7 +420,7 @@
 
 def body(field, cotangent, spectral_weight, first_moment, second_moment, local_weight):
     left_x, right_x, half_x, right_y, left_y, left_z, right_z, order, order_t = constants()
-    received = exchange(forward(field, left_x, left_y))
+    received = exchange(forward(field, left_x, right_y))
     local = local_mix(field, local_weight)
     spread = spread_weights(spectral_weight, order, order_t)
     received, local, spread = lax.optimization_barrier((received, local, spread))

time: 106 us -> 105 us (level)
  no operation moved by 1% of the time
where the time goes in v5:
time: 105 us
  blocking collectives  51.7 us (49%)
  Pallas kernels  23.2 us (22%)
  starting transfers between devices  16.7 us (16%)
  waiting for transfers between devices  12.4 us (12%)
    all_to_all x2, blocking collectives, exchange(): lax.all_to_all(messages, ('dp', 'mp'), split_axis=0, concat_axis=0, tiled...  51.7 us
    all_to_all x1, starting transfers between devices, exchange(): lax.all_to_all(messages, ('dp', 'mp'), split_axis=0, concat_axis=0, tiled...  16.7 us
    all_to_all x1, waiting for transfers between devices, exchange(): lax.all_to_all(messages, ('dp', 'mp'), split_axis=0, concat_axis=0, tiled...  12.4 us
    pallas_call x1, Pallas kernels, local_mix(): call(local_kernel, 4, [plane, whole((32, 32))], plane, jax.ShapeDtypeStru...  5.89 us
    pallas_call x1, Pallas kernels, forward(): call(forward_kernel, 1, [outside()] * 3, whole(MESSAGES), jax.ShapeDtypeS...  4.99 us
    pallas_call x1, Pallas kernels, middle(): call(middle_kernel, 1, [whole(MESSAGES), resident(), resident(), whole((1...  4.32 us
    pallas_call x1, Pallas kernels, update(): call(update_kernel, 1, [whole((2048, 128)), whole((512, 128)), whole((128...  4.02 us
    pallas_call x1, Pallas kernels, mix(): call(mix_kernel, 1, [whole((2048, 128)), whole((32, 128, 128)), whole((12...  2.28 us
  transfers between devices with their start and end apart: 1, of which 1 were waited for; matrix products, arithmetic and copies ran while one was open for 0% of the time, Pallas kernels for 7%

profile of v5, /device:TPU:1, one launch (start us, length us, event | category | flops | bytes accessed | tf_op | source)
XLA Modules:
  0.0 104.9 jit_solution(6781429643961091529)
XLA Ops:
  0.6 0.0 copy-start.4
  0.6 0.0 copy-start.6
  0.7 0.0 copy-start
  0.7 5.0 %planes_to_modes.1 = bf16[16,8,16,128]{3,2,1,0:T(8,128)(2,1)} custom-call(bf16[1,32,8,64,128]{4,3,2,1,0:T(8,128)(2,1)} %field.3, bf16[128,256]{1,0:T(8,128)(2,1)} %constant.18.clone.left_x, bf16[512,128]{1,0:T(8,128)(2,1)} %constant.21.clone.right_y), custom_call_target="tpu_custom_call" | custom-call | flops 2147483648 | bytes 8388608 | tf_op jit(solution)/shard_map/planes_to_modes/pallas_call | solution.py:135
  5.7 16.7 %all-to-all-start = ((bf16[256,8,128]{2,1,0:T(8,128)(2,1)}), bf16[256,8,128]{2,1,0:T(8,128)(2,1)}, u32[]{:S(2)}, u32[]{:S(2)}) async-start(bf16[256,8,128]{2,1,0:T(8,128)(2,1)} %bitcast.10), calls=%async_computation | async-start | bytes 1048576 | tf_op jit(solution)/shard_map/all_to_all | solution.py:418
  22.3 0.0 copy-done.4
  22.3 0.0 copy-done.6
  22.4 0.0 copy-done
  22.4 1.7 %spread_weights.1.weights = bf16[32,128,128]{2,1,0:T(8,128)(2,1)S(1)} custom-call(f32[2,2,32,32,32]{4,3,2,1,0:T(8,128)S(1)} %copy-done, bf16[128,128]{1,0:T(8,128)(2,1)S(1)} %copy-done.6, bf16[128,128]{1,0:T(8,128)(2,1)S(1)} %copy-done.4), custom_call_target="tpu_custom_call" | custom-call | flops 268435456 | bytes 8388608 | tf_op jit(solution)/shard_map/spread_weights/pallas_call | solution.py:209
  24.1 0.0 copy-start.5
  24.1 0.0 copy-start.12
  24.1 5.9 %local_mix.1.local = bf16[1,32,8,64,128]{4,3,2,1,0:T(8,128)(2,1)} custom-call(bf16[1,32,8,64,128]{4,3,2,1,0:T(8,128)(2,1)} %field.3, bf16[32,32]{1,0:T(8,128)(2,1)} %weight.3), custom_call_target="tpu_custom_call" | custom-call | flops 2147483648 | bytes 8388608 | tf_op jit(solution)/shard_map/local_mix/pallas_call | solution.py:183
  30.0 12.4 %all-to-all-done = bf16[256,8,128]{2,1,0:T(8,128)(2,1)} async-done(((bf16[256,8,128]{2,1,0:T(8,128)(2,1)}), bf16[256,8,128]{2,1,0:T(8,128)(2,1)}, u32[]{:S(2)}, u32[]{:S(2)}) %all-to-all-start) | async-done | bytes 524320 | tf_op jit(solution)/shard_map/all_to_all | solution.py:418
  42.5 0.0 copy-done.5
  42.5 0.0 copy-done.12
  42.5 0.0 copy-start.1
  42.5 0.0 copy-start.7
  42.5 0.0 copy-start.8
  42.5 0.0 copy-start.9
  42.5 0.0 copy-start.10
  42.5 0.0 copy-start.11
  42.5 2.3 %mix_modes.1 = (bf16[2048,128]{1,0:T(8,128)(2,1)S(1)}, bf16[512,128]{1,0:T(8,128)(2,1)S(1)}) custom-call(bf16[2048,128]{1,0:T(8,128)(2,1)} %bitcast.1.received, bf16[32,128,128]{2,1,0:T(8,128)(2,1)S(1)} %spread_weights.1.weights, bf16[128,128]{1,0:T(8,128)(2,1)S(1)} %copy-done.5, bf16[128,128]{1,0:T(8,128)(2,1)S(1)} %copy-done.12), custom_call_target="tpu_custom_call" | custom-call | flops 17179869184 | bytes 8388608 | tf_op jit(solution)/shard_map/mix_modes/pallas_call | solution.py:260
  44.8 25.8 %all_to_all.32 = bf16[256,8,128]{2,1,0:T(8,128)(2,1)S(1)} all-to-all(bf16[256,8,128]{2,1,0:T(8,128)(2,1)S(1)} %bitcast.9), channel_id=1, replica_groups=mesh['dp'=16,'mp'=16] {'dp','mp'}, dimensions={0} | all-to-all | bytes 1048576 | tf_op jit(solution)/shard_map/all_to_all | solution.py:418
  70.7 0.0 copy-done.1
  70.7 0.0 copy-done.7
  70.7 0.0 copy-done.8
  70.7 0.0 copy-done.9
  70.7 0.0 copy-done.10
  70.7 0.0 copy-done.11
  70.7 0.0 copy-start.2
  70.7 0.0 copy-start.3
  70.7 4.3 %gelu_gradient.1 = bf16[16,8,16,128]{3,2,1,0:T(8,128)(2,1)S(1)} custom-call(bf16[16,8,16,128]{3,2,1,0:T(8,128)(2,1)S(1)} %bitcast.7, bf16[1,32,8,64,128]{4,3,2,1,0:T(8,128)(2,1)S(1)} %copy-done.1, bf16[1,32,8,64,128]{4,3,2,1,0:T(8,128)(2,1)S(1)} %copy-done.7, bf16[128,256]{1,0:T(8,128)(2,1)S(1)} %copy-done.10, bf16[256,128]{1,0:T(8,128)(2,1)S(1)} %copy-done.11, ...), custom_call_target="tpu_custom_call" | custom-call | flops 4294967296 | bytes 8388608 | tf_op jit(solution)/shard_map/gelu_gradient/pallas_call | solution.py:322
  75.1 25.8 %all_to_all.33 = bf16[256,8,128]{2,1,0:T(8,128)(2,1)S(1)} all-to-all(bf16[256,8,128]{2,1,0:T(8,128)(2,1)S(1)} %bitcast.8), channel_id=1, replica_groups=mesh['dp'=16,'mp'=16] {'dp','mp'}, dimensions={0} | all-to-all | bytes 1048576 | tf_op jit(solution)/shard_map/all_to_all | solution.py:418
  100.9 0.0 copy-done.2
  100.9 0.0 copy-done.3
  100.9 4.0 %adam_update.1 = (f32[2,2,32,32,32]{4,3,2,1,0:T(8,128)}, f32[2,2,32,32,32]{4,3,2,1,0:T(8,128)}, f32[2,2,32,32,32]{4,3,2,1,0:T(8,128)}) custom-call(bf16[2048,128]{1,0:T(8,128)(2,1)S(1)} %bitcast.6, bf16[512,128]{1,0:T(8,128)(2,1)S(1)} %get-tuple-element.12.kept, bf16[128,128]{1,0:T(8,128)(2,1)S(1)} %copy-done.5, bf16[128,128]{1,0:T(8,128)(2,1)S(1)} %copy-done.4, ...), custom_call_target="tpu_custom_call" | custom-call | flops 268435456 | bytes 8388608 | tf_op jit(solution)/shard_map/adam_update/pallas_call | solution.py:400
Async XLA Ops:
  0.6 21.7 %copy-start.4 = (bf16[128,128]{1,0:T(8,128)(2,1)S(1)}, bf16[128,128]{1,0:T(8,128)(2,1)}, u32[]{:S(2)}) copy-start(bf16[128,128]{1,0:T(8,128)(2,1)} %constant.26.clone.order_t) | copy-start | bytes 98308
  0.6 21.7 %copy-start.6 = (bf16[128,128]{1,0:T(8,128)(2,1)S(1)}, bf16[128,128]{1,0:T(8,128)(2,1)}, u32[]{:S(2)}) copy-start(bf16[128,128]{1,0:T(8,128)(2,1)} %constant.25.clone.order) | copy-start | bytes 98308
  0.7 21.7 %copy-start = (f32[2,2,32,32,32]{4,3,2,1,0:T(8,128)S(1)}, f32[2,2,32,32,32]{4,3,2,1,0:T(8,128)}, u32[]{:S(2)}) copy-start(f32[2,2,32,32,32]{4,3,2,1,0:T(8,128)} %weight.5) | copy-start | bytes 1572868
  5.7 36.8 %all-to-all-start = ((bf16[256,8,128]{2,1,0:T(8,128)(2,1)}), bf16[256,8,128]{2,1,0:T(8,128)(2,1)}, u32[]{:S(2)}, u32[]{:S(2)}) async-start(bf16[256,8,128]{2,1,0:T(8,128)(2,1)} %bitcast.10), calls=%async_computation | async-start | bytes 1048576 | tf_op jit(solution)/shard_map/all_to_all | solution.py:418
  24.1 18.4 %copy-start.5 = (bf16[128,128]{1,0:T(8,128)(2,1)S(1)}, bf16[128,128]{1,0:T(8,128)(2,1)}, u32[]{:S(2)}) copy-start(bf16[128,128]{1,0:T(8,128)(2,1)} %constant.23.clone.left_z) | copy-start | bytes 98308
  24.1 18.3 %copy-start.12 = (bf16[128,128]{1,0:T(8,128)(2,1)S(1)}, bf16[128,128]{1,0:T(8,128)(2,1)}, u32[]{:S(2)}) copy-start(bf16[128,128]{1,0:T(8,128)(2,1)} %constant.24.clone.right_z) | copy-start | bytes 98308
  42.5 28.2 %copy-start.1 = (bf16[1,32,8,64,128]{4,3,2,1,0:T(8,128)(2,1)S(1)}, bf16[1,32,8,64,128]{4,3,2,1,0:T(8,128)(2,1)}, u32[]{:S(2)}) copy-start(bf16[1,32,8,64,128]{4,3,2,1,0:T(8,128)(2,1)} %local_mix.1.local) | copy-start | bytes 12582916
  42.5 28.2 %copy-start.7 = (bf16[1,32,8,64,128]{4,3,2,1,0:T(8,128)(2,1)S(1)}, bf16[1,32,8,64,128]{4,3,2,1,0:T(8,128)(2,1)}, u32[]{:S(2)}) copy-start(bf16[1,32,8,64,128]{4,3,2,1,0:T(8,128)(2,1)} %cot.1) | copy-start | bytes 12582916
  42.5 28.2 %copy-start.8 = (bf16[512,128]{1,0:T(8,128)(2,1)S(1)}, bf16[512,128]{1,0:T(8,128)(2,1)}, u32[]{:S(2)}) copy-start(bf16[512,128]{1,0:T(8,128)(2,1)} %constant.21.clone.right_y) | copy-start | bytes 393220
  42.5 28.2 %copy-start.9 = (bf16[128,512]{1,0:T(8,128)(2,1)S(1)}, bf16[128,512]{1,0:T(8,128)(2,1)}, u32[]{:S(2)}) copy-start(bf16[128,512]{1,0:T(8,128)(2,1)} %constant.22.clone.left_y) | copy-start | bytes 393220
  42.5 28.2 %copy-start.10 = (bf16[128,256]{1,0:T(8,128)(2,1)S(1)}, bf16[128,256]{1,0:T(8,128)(2,1)}, u32[]{:S(2)}) copy-start(bf16[128,256]{1,0:T(8,128)(2,1)} %constant.20.clone.half_x) | copy-start | bytes 196612
  42.5 28.2 %copy-start.11 = (bf16[256,128]{1,0:T(8,128)(2,1)S(1)}, bf16[256,128]{1,0:T(8,128)(2,1)}, u32[]{:S(2)}) copy-start(bf16[256,128]{1,0:T(8,128)(2,1)} %constant.19.clone.right_x) | copy-start | bytes 196612
  70.7 30.2 %copy-start.2 = (f32[2,2,32,32,32]{4,3,2,1,0:T(8,128)S(1)}, f32[2,2,32,32,32]{4,3,2,1,0:T(8,128)}, u32[]{:S(2)}) copy-start(f32[2,2,32,32,32]{4,3,2,1,0:T(8,128)} %moment.1) | copy-start | bytes 1572868
  70.7 30.2 %copy-start.3 = (f32[2,2,32,32,32]{4,3,2,1,0:T(8,128)S(1)}, f32[2,2,32,32,32]{4,3,2,1,0:T(8,128)}, u32[]{:S(2)}) copy-start(f32[2,2,32,32,32]{4,3,2,1,0:T(8,128)} %second.1) | copy-start | bytes 1572868

commit v6 on v5

--- a/solution.py
+++ b/solution.py
@@ -219,9 +219,11 @@
     )(weight, order, order_t)
 
 
-def z_modes(received, left_z, spectrum):
+def z_modes(received, left_z, spectrum, pieces=()):
     low_half = lax.broadcasted_iota(jnp.int32, (32, 128), 1) < 64
     for pair in range(8):
+        if pieces and pair % 2 == 0:
+            pieces[pair // 2].wait()
         both = [received[s * 128 : (s + 1) * 128, :] for s in (2 * pair, 2 * pair + 1)]
         product = dot(left_z, jnp.concatenate(both, axis=1))
         for odd in range(2):
@@ -231,8 +233,14 @@
             spectrum[pl.ds(2 * pair + odd, 32, stride=16), :] = stay + pltpu.roll(move, 64, axis=1)
 
 
-def mix_kernel(received, weights, left_z, right_z, out, kept, spectrum, mixed):
-    z_modes(received, left_z[...], spectrum)
+def mix_kernel(received, weights, left_z, right_z, out, kept, buffer, spectrum, mixed, sems):
+    pieces = []
+    for i in range(4):
+        rows = pl.ds(i * 512, 512)
+        pieces.append(pltpu.make_async_copy(received.at[rows], buffer.at[rows], sems.at[i]))
+    for piece in pieces:
+        piece.start()
+    z_modes(buffer, left_z[...], spectrum, pieces)
     kept[...] = spectrum[...].astype(BF16)
     for k in range(32):
         rows = slice(k * 16, (k + 1) * 16)
@@ -260,10 +268,15 @@
     return call(
         mix_kernel,
         1,
-        [whole((2048, 128)), whole((32, 128, 128)), whole((128, 128)), whole((128, 128))],
+        [outside(), whole((32, 128, 128)), whole((128, 128)), whole((128, 128))],
         [whole((2048, 128)), whole((512, 128))],
         [jax.ShapeDtypeStruct((2048, 128), BF16), jax.ShapeDtypeStruct((512, 128), BF16)],
-        [pltpu.VMEM((512, 128), F32), pltpu.VMEM((512, 128), F32)],
+        [
+            pltpu.VMEM((2048, 128), BF16),
+            pltpu.VMEM((512, 128), F32),
+            pltpu.VMEM((512, 128), F32),
+            pltpu.SemaphoreType.DMA((4,)),
+        ],
         1 << 34,
         "mix_modes",
         16,

time: 105 us -> 106 us (level)
  no operation moved by 1% of the time
where the time goes in v6:
time: 106 us; the launch traced here: 105 us
  blocking collectives  51.7 us (49%)
  Pallas kernels  23.8 us (22%)
  starting transfers between devices  16.7 us (16%)
  waiting for transfers between devices  12.4 us (12%)
    all_to_all x2, blocking collectives, exchange(): lax.all_to_all(messages, ('dp', 'mp'), split_axis=0, concat_axis=0, tiled...  51.7 us
    all_to_all x1, starting transfers between devices, exchange(): lax.all_to_all(messages, ('dp', 'mp'), split_axis=0, concat_axis=0, tiled...  16.7 us
    all_to_all x1, waiting for transfers between devices, exchange(): lax.all_to_all(messages, ('dp', 'mp'), split_axis=0, concat_axis=0, tiled...  12.4 us
    pallas_call x1, Pallas kernels, local_mix(): call(local_kernel, 4, [plane, whole((32, 32))], plane, jax.ShapeDtypeStru...  5.89 us
    pallas_call x1, Pallas kernels, forward(): call(forward_kernel, 1, [outside()] * 3, whole(MESSAGES), jax.ShapeDtypeS...  4.99 us
    pallas_call x1, Pallas kernels, middle(): call(middle_kernel, 1, [whole(MESSAGES), resident(), resident(), whole((1...  4.32 us
    pallas_call x1, Pallas kernels, update(): call(update_kernel, 1, [whole((2048, 128)), whole((512, 128)), whole((128...  4.02 us
    pallas_call x1, Pallas kernels, mix(): call(mix_kernel, 1, [outside(), whole((32, 128, 128)), whole((128, 128)),...  2.81 us
  transfers between devices with their start and end apart: 1, of which 1 were waited for; matrix products, arithmetic and copies ran while one was open for 0% of the time, Pallas kernels for 7%

profile of v6, /device:TPU:1, one launch (start us, length us, event | category | flops | bytes accessed | tf_op | source)
XLA Modules:
  0.0 105.4 jit_solution(12263033460047564837)
XLA Ops:
  0.6 0.0 copy-start.4
  0.6 0.0 copy-start.6
  0.7 0.0 copy-start
  0.7 5.0 %planes_to_modes.1 = bf16[16,8,16,128]{3,2,1,0:T(8,128)(2,1)} custom-call(bf16[1,32,8,64,128]{4,3,2,1,0:T(8,128)(2,1)} %field.3, bf16[128,256]{1,0:T(8,128)(2,1)} %constant.18.clone.left_x, bf16[512,128]{1,0:T(8,128)(2,1)} %constant.21.clone.right_y), custom_call_target="tpu_custom_call" | custom-call | flops 2147483648 | bytes 8388608 | tf_op jit(solution)/shard_map/planes_to_modes/pallas_call | solution.py:135
  5.7 16.7 %all-to-all-start = ((bf16[256,8,128]{2,1,0:T(8,128)(2,1)}), bf16[256,8,128]{2,1,0:T(8,128)(2,1)}, u32[]{:S(2)}, u32[]{:S(2)}) async-start(bf16[256,8,128]{2,1,0:T(8,128)(2,1)} %bitcast.10), calls=%async_computation | async-start | bytes 1048576 | tf_op jit(solution)/shard_map/all_to_all | solution.py:431
  22.3 0.0 copy-done.4
  22.3 0.0 copy-done.6
  22.4 0.0 copy-done
  22.4 1.7 %spread_weights.1.weights = bf16[32,128,128]{2,1,0:T(8,128)(2,1)S(1)} custom-call(f32[2,2,32,32,32]{4,3,2,1,0:T(8,128)S(1)} %copy-done, bf16[128,128]{1,0:T(8,128)(2,1)S(1)} %copy-done.6, bf16[128,128]{1,0:T(8,128)(2,1)S(1)} %copy-done.4), custom_call_target="tpu_custom_call" | custom-call | flops 268435456 | bytes 8388608 | tf_op jit(solution)/shard_map/spread_weights/pallas_call | solution.py:209
  24.1 0.0 copy-start.5
  24.1 0.0 copy-start.12
  24.1 5.9 %local_mix.1.local = bf16[1,32,8,64,128]{4,3,2,1,0:T(8,128)(2,1)} custom-call(bf16[1,32,8,64,128]{4,3,2,1,0:T(8,128)(2,1)} %field.3, bf16[32,32]{1,0:T(8,128)(2,1)} %weight.3), custom_call_target="tpu_custom_call" | custom-call | flops 2147483648 | bytes 8388608 | tf_op jit(solution)/shard_map/local_mix/pallas_call | solution.py:183
  30.0 12.4 %all-to-all-done = bf16[256,8,128]{2,1,0:T(8,128)(2,1)} async-done(((bf16[256,8,128]{2,1,0:T(8,128)(2,1)}), bf16[256,8,128]{2,1,0:T(8,128)(2,1)}, u32[]{:S(2)}, u32[]{:S(2)}) %all-to-all-start) | async-done | bytes 524320 | tf_op jit(solution)/shard_map/all_to_all | solution.py:431
  42.5 0.0 copy-done.5
  42.5 0.0 copy-done.12
  42.5 0.0 copy-start.1
  42.5 0.0 copy-start.7
  42.5 0.0 copy-start.8
  42.5 0.0 copy-start.9
  42.5 0.0 copy-start.10
  42.5 0.0 copy-start.11
  42.5 2.8 %mix_modes.1 = (bf16[2048,128]{1,0:T(8,128)(2,1)S(1)}, bf16[512,128]{1,0:T(8,128)(2,1)S(1)}) custom-call(bf16[2048,128]{1,0:T(8,128)(2,1)} %bitcast.1.received, bf16[32,128,128]{2,1,0:T(8,128)(2,1)S(1)} %spread_weights.1.weights, bf16[128,128]{1,0:T(8,128)(2,1)S(1)} %copy-done.5, bf16[128,128]{1,0:T(8,128)(2,1)S(1)} %copy-done.12), custom_call_target="tpu_custom_call" | custom-call | flops 17179869184 | bytes 8388608 | tf_op jit(solution)/shard_map/mix_modes/pallas_call | solution.py:268
  45.4 25.8 %all_to_all.32 = bf16[256,8,128]{2,1,0:T(8,128)(2,1)S(1)} all-to-all(bf16[256,8,128]{2,1,0:T(8,128)(2,1)S(1)} %bitcast.9), channel_id=1, replica_groups=mesh['dp'=16,'mp'=16] {'dp','mp'}, dimensions={0} | all-to-all | bytes 1048576 | tf_op jit(solution)/shard_map/all_to_all | solution.py:431
  71.2 0.0 copy-done.1
  71.2 0.0 copy-done.7
  71.2 0.0 copy-done.8
  71.2 0.0 copy-done.9
  71.2 0.0 copy-done.10
  71.2 0.0 copy-done.11
  71.2 0.0 copy-start.2
  71.2 0.0 copy-start.3
  71.3 4.3 %gelu_gradient.1 = bf16[16,8,16,128]{3,2,1,0:T(8,128)(2,1)S(1)} custom-call(bf16[16,8,16,128]{3,2,1,0:T(8,128)(2,1)S(1)} %bitcast.7, bf16[1,32,8,64,128]{4,3,2,1,0:T(8,128)(2,1)S(1)} %copy-done.1, bf16[1,32,8,64,128]{4,3,2,1,0:T(8,128)(2,1)S(1)} %copy-done.7, bf16[128,256]{1,0:T(8,128)(2,1)S(1)} %copy-done.10, bf16[256,128]{1,0:T(8,128)(2,1)S(1)} %copy-done.11, ...), custom_call_target="tpu_custom_call" | custom-call | flops 4294967296 | bytes 8388608 | tf_op jit(solution)/shard_map/gelu_gradient/pallas_call | solution.py:335
  75.6 25.8 %all_to_all.33 = bf16[256,8,128]{2,1,0:T(8,128)(2,1)S(1)} all-to-all(bf16[256,8,128]{2,1,0:T(8,128)(2,1)S(1)} %bitcast.8), channel_id=1, replica_groups=mesh['dp'=16,'mp'=16] {'dp','mp'}, dimensions={0} | all-to-all | bytes 1048576 | tf_op jit(solution)/shard_map/all_to_all | solution.py:431
  101.4 0.0 copy-done.2
  101.4 0.0 copy-done.3
  101.4 4.0 %adam_update.1 = (f32[2,2,32,32,32]{4,3,2,1,0:T(8,128)}, f32[2,2,32,32,32]{4,3,2,1,0:T(8,128)}, f32[2,2,32,32,32]{4,3,2,1,0:T(8,128)}) custom-call(bf16[2048,128]{1,0:T(8,128)(2,1)S(1)} %bitcast.6, bf16[512,128]{1,0:T(8,128)(2,1)S(1)} %get-tuple-element.12.kept, bf16[128,128]{1,0:T(8,128)(2,1)S(1)} %copy-done.5, bf16[128,128]{1,0:T(8,128)(2,1)S(1)} %copy-done.4, ...), custom_call_target="tpu_custom_call" | custom-call | flops 268435456 | bytes 8388608 | tf_op jit(solution)/shard_map/adam_update/pallas_call | solution.py:413
Async XLA Ops:
  0.6 21.7 %copy-start.4 = (bf16[128,128]{1,0:T(8,128)(2,1)S(1)}, bf16[128,128]{1,0:T(8,128)(2,1)}, u32[]{:S(2)}) copy-start(bf16[128,128]{1,0:T(8,128)(2,1)} %constant.26.clone.order_t) | copy-start | bytes 98308
  0.6 21.7 %copy-start.6 = (bf16[128,128]{1,0:T(8,128)(2,1)S(1)}, bf16[128,128]{1,0:T(8,128)(2,1)}, u32[]{:S(2)}) copy-start(bf16[128,128]{1,0:T(8,128)(2,1)} %constant.25.clone.order) | copy-start | bytes 98308
  0.7 21.7 %copy-start = (f32[2,2,32,32,32]{4,3,2,1,0:T(8,128)S(1)}, f32[2,2,32,32,32]{4,3,2,1,0:T(8,128)}, u32[]{:S(2)}) copy-start(f32[2,2,32,32,32]{4,3,2,1,0:T(8,128)} %weight.5) | copy-start | bytes 1572868
  5.7 36.8 %all-to-all-start = ((bf16[256,8,128]{2,1,0:T(8,128)(2,1)}), bf16[256,8,128]{2,1,0:T(8,128)(2,1)}, u32[]{:S(2)}, u32[]{:S(2)}) async-start(bf16[256,8,128]{2,1,0:T(8,128)(2,1)} %bitcast.10), calls=%async_computation | async-start | bytes 1048576 | tf_op jit(solution)/shard_map/all_to_all | solution.py:431
  24.1 18.4 %copy-start.5 = (bf16[128,128]{1,0:T(8,128)(2,1)S(1)}, bf16[128,128]{1,0:T(8,128)(2,1)}, u32[]{:S(2)}) copy-start(bf16[128,128]{1,0:T(8,128)(2,1)} %constant.23.clone.left_z) | copy-start | bytes 98308
  24.1 18.3 %copy-start.12 = (bf16[128,128]{1,0:T(8,128)(2,1)S(1)}, bf16[128,128]{1,0:T(8,128)(2,1)}, u32[]{:S(2)}) copy-start(bf16[128,128]{1,0:T(8,128)(2,1)} %constant.24.clone.right_z) | copy-start | bytes 98308
  42.5 28.7 %copy-start.1 = (bf16[1,32,8,64,128]{4,3,2,1,0:T(8,128)(2,1)S(1)}, bf16[1,32,8,64,128]{4,3,2,1,0:T(8,128)(2,1)}, u32[]{:S(2)}) copy-start(bf16[1,32,8,64,128]{4,3,2,1,0:T(8,128)(2,1)} %local_mix.1.local) | copy-start | bytes 12582916
  42.5 28.7 %copy-start.7 = (bf16[1,32,8,64,128]{4,3,2,1,0:T(8,128)(2,1)S(1)}, bf16[1,32,8,64,128]{4,3,2,1,0:T(8,128)(2,1)}, u32[]{:S(2)}) copy-start(bf16[1,32,8,64,128]{4,3,2,1,0:T(8,128)(2,1)} %cot.1) | copy-start | bytes 12582916
  42.5 28.7 %copy-start.8 = (bf16[512,128]{1,0:T(8,128)(2,1)S(1)}, bf16[512,128]{1,0:T(8,128)(2,1)}, u32[]{:S(2)}) copy-start(bf16[512,128]{1,0:T(8,128)(2,1)} %constant.21.clone.right_y) | copy-start | bytes 393220
  42.5 28.7 %copy-start.9 = (bf16[128,512]{1,0:T(8,128)(2,1)S(1)}, bf16[128,512]{1,0:T(8,128)(2,1)}, u32[]{:S(2)}) copy-start(bf16[128,512]{1,0:T(8,128)(2,1)} %constant.22.clone.left_y) | copy-start | bytes 393220
  42.5 28.7 %copy-start.10 = (bf16[128,256]{1,0:T(8,128)(2,1)S(1)}, bf16[128,256]{1,0:T(8,128)(2,1)}, u32[]{:S(2)}) copy-start(bf16[128,256]{1,0:T(8,128)(2,1)} %constant.20.clone.half_x) | copy-start | bytes 196612
  42.5 28.7 %copy-start.11 = (bf16[256,128]{1,0:T(8,128)(2,1)S(1)}, bf16[256,128]{1,0:T(8,128)(2,1)}, u32[]{:S(2)}) copy-start(bf16[256,128]{1,0:T(8,128)(2,1)} %constant.19.clone.right_x) | copy-start | bytes 196612
  71.2 30.2 %copy-start.2 = (f32[2,2,32,32,32]{4,3,2,1,0:T(8,128)S(1)}, f32[2,2,32,32,32]{4,3,2,1,0:T(8,128)}, u32[]{:S(2)}) copy-start(f32[2,2,32,32,32]{4,3,2,1,0:T(8,128)} %moment.1) | copy-start | bytes 1572868
  71.2 30.2 %copy-start.3 = (f32[2,2,32,32,32]{4,3,2,1,0:T(8,128)S(1)}, f32[2,2,32,32,32]{4,3,2,1,0:T(8,128)}, u32[]{:S(2)}) copy-start(f32[2,2,32,32,32]{4,3,2,1,0:T(8,128)} %second.1) | copy-start | bytes 1572868
